TPU v7x, 32 devices: a whole 2x2x4 slice. The times are simulated.
32 devices in a mesh: gx: 4 (over y, core), gy: 2 (over x), gz: 4 (over z).
Axes of the slice: x: 2, y: 2, z: 4, core: 2. Of those that a mesh axis runs over, the one named last changes fastest.
Arguments:
- source: float32 [32, 64, 512], P('gx', 'gy', 'gz'), may hold values from -24 to 24
- conductivity: float32 [32, 64, 512], P('gx', 'gy', 'gz'), may hold values from 0.2 to 5
Outputs:
- pressure: float32 [32, 64, 512], P('gx', 'gy', 'gz')
All inputs are finite; a program needn't handle non-finite values.
Results may differ from a plain program's by a relative error of at most 0.00002.
Values sent between devices are 32-bit elements; how exact they have to be, the bound alone decides.
A program may use at most 64 MiB of HBM per device.

v0:
```python
import math

import jax
import jax.numpy as jnp
from jax import lax
from jax.sharding import PartitionSpec as P

spectrum_top = 1.9
spectrum_low = 0.475
omega_first = 1.0 / (
    (spectrum_top + spectrum_low) / 2 + (spectrum_top - spectrum_low) / 2 * math.cos(math.pi / 4)
)
omega_second = 1.0 / (
    (spectrum_top + spectrum_low) / 2
    + (spectrum_top - spectrum_low) / 2 * math.cos(3 * math.pi / 4)
)
face_pairs = ((0, 1), (0, -1), (1, 1), (1, -1), (2, 1), (2, -1))


def padded_2(cells, sides, width):
    for axis, dim in sides:
        count = lax.axis_size(axis)
        ends = count - 1
        head = lax.slice_in_dim(cells, 0, width, axis=dim)
        tail = lax.slice_in_dim(cells, cells.shape[dim] - width, cells.shape[dim], axis=dim)
        cells = jnp.concatenate(
            [
                lax.ppermute(tail, axis, [(i, (i + 1) % count) for i in range(ends)]),
                cells,
                lax.ppermute(head, axis, [((i + 1) % count, i) for i in range(ends)]),
            ],
            axis=dim,
        )
    return cells


def from_partner(block, axis, stride):
    count = lax.axis_size(axis)
    route = []
    for low in range(count):
        high = low | 1 << stride
        if high != low and high < count:
            route += [(low, high), (high, low)]
    return lax.ppermute(block, axis, route)


def interior(padded):
    return padded[1:-1, 1:-1, 1:-1]


def neighbour(padded, dimension, offset):
    starts = [1, 1, 1]
    limits = [padded.shape[0] - 1, padded.shape[1] - 1, padded.shape[2] - 1]
    starts[dimension] = 1 + offset
    limits[dimension] = padded.shape[dimension] - 1 + offset
    return lax.slice(padded, tuple(starts), tuple(limits))


def diagonal_of(coeff_pad):
    centre = interior(coeff_pad)
    result = jnp.zeros_like(centre)
    for dimension, offset in face_pairs:
        result = result + 0.5 * (centre + neighbour(coeff_pad, dimension, offset))
    return result


def operate(field_pad, coeff_pad):
    centre = interior(coeff_pad)
    values = interior(field_pad)
    result = jnp.zeros_like(centre)
    for dimension, offset in face_pairs:
        weight = 0.5 * (centre + neighbour(coeff_pad, dimension, offset))
        result = result + weight * (values - neighbour(field_pad, dimension, offset))
    return result


def sweep(field, field_pad, coeff_pad, rhs_field, diagonal, omega_value):
    return field + omega_value * (rhs_field - operate(field_pad, coeff_pad)) / diagonal


def restrict_axis(values, dimension):
    cells = (values.shape[dimension] - 2) // 2
    pieces = [
        lax.slice_in_dim(values, start_cell, start_cell + 2 * cells - 1, stride=2, axis=dimension)
        for start_cell in range(4)
    ]
    return (pieces[0] + 3.0 * pieces[1] + 3.0 * pieces[2] + pieces[3]) * 0.125


def restrict(padded):
    return restrict_axis(restrict_axis(restrict_axis(padded, 0), 1), 2)


def interpolate_axis(values, dimension):
    cells = values.shape[dimension] - 2
    lower_side = lax.slice_in_dim(values, 0, cells, axis=dimension)
    centre = lax.slice_in_dim(values, 1, cells + 1, axis=dimension)
    upper_side = lax.slice_in_dim(values, 2, cells + 2, axis=dimension)
    even_cells = 0.75 * centre + 0.25 * lower_side
    odd_cells = 0.75 * centre + 0.25 * upper_side
    paired = jnp.stack([even_cells, odd_cells], axis=dimension + 1)
    new_shape = list(values.shape)
    new_shape[dimension] = 2 * cells
    return paired.reshape(tuple(new_shape))


def interpolate(padded):
    return interpolate_axis(interpolate_axis(interpolate_axis(padded, 0), 1), 2)


def coarsen(values):
    first, second, third = values.shape
    return values.reshape(first // 2, 2, second // 2, 2, third // 2, 2).mean(axis=(1, 3, 5))


def pad_zero(values):
    return jnp.pad(values, 1)


def box_correction(coeff_box, rhs_box):
    coeff_pad = pad_zero(coeff_box)
    diagonal = diagonal_of(coeff_pad)
    field = omega_first * rhs_box / diagonal
    field = sweep(field, pad_zero(field), coeff_pad, rhs_box, diagonal, omega_second)
    return interpolate(pad_zero(field))


def fine_halo(values):
    return padded_2(values, (("gx", 0), ("gy", 1), ("gz", 2)), 1)


def middle_halo(values):
    return padded_2(values, (("gx", 0), ("gy", 1), ("gz", 2)), 1)


def parities():
    return (lax.axis_index("gx") % 2, lax.axis_index("gy") % 2, lax.axis_index("gz") % 2)


def gathered_correction(coarse_coeff, coarse_rhs):
    parity_first, parity_second, parity_third = parities()
    third_bits = lax.axis_size("gz").bit_length() - 1
    second_bits = lax.axis_size("gy").bit_length() - 1
    stacked = jnp.stack([coarse_coeff, coarse_rhs])
    for dimension, bit_index, parity in (
        (3, 0, parity_third),
        (2, third_bits, parity_second),
        (1, third_bits + second_bits, parity_first),
    ):
        partner = from_partner(stacked, ("gx", "gy", "gz"), bit_index)
        upper_half = parity == 1
        lower_part = jnp.where(upper_half, partner, stacked)
        upper_part = jnp.where(upper_half, stacked, partner)
        stacked = jnp.concatenate([lower_part, upper_part], axis=dimension)
    box_field = box_correction(stacked[0], stacked[1])
    block_shape = tuple((2 * extent for extent in coarse_coeff.shape))
    anchors = (
        parity_first * block_shape[0],
        parity_second * block_shape[1],
        parity_third * block_shape[2],
    )
    return lax.dynamic_slice(box_field, anchors, block_shape)


def local(source, conductivity):
    coeff_pad = fine_halo(conductivity)
    fine_diag = diagonal_of(coeff_pad)
    pressure = omega_first * source / fine_diag
    pressure = sweep(pressure, fine_halo(pressure), coeff_pad, source, fine_diag, omega_second)
    leftover = source - operate(fine_halo(pressure), coeff_pad)
    middle_rhs = 4.0 * restrict(fine_halo(leftover))
    middle_coeff = coarsen(conductivity)
    middle_pad = middle_halo(middle_coeff)
    middle_diag = diagonal_of(middle_pad)
    middle = omega_first * middle_rhs / middle_diag
    middle = sweep(middle, middle_halo(middle), middle_pad, middle_rhs, middle_diag, omega_second)
    middle_left = middle_rhs - operate(middle_halo(middle), middle_pad)
    coarse_rhs = 4.0 * restrict(middle_halo(middle_left))
    coarse_coeff = coarsen(middle_coeff)
    correction = gathered_correction(coarse_coeff, coarse_rhs)
    middle = middle + correction
    for omega_value in (omega_first, omega_second):
        middle = sweep(
            middle, middle_halo(middle), middle_pad, middle_rhs, middle_diag, omega_value
        )
    pressure = pressure + interpolate(middle_halo(middle))
    for omega_value in (omega_first, omega_second):
        pressure = sweep(pressure, fine_halo(pressure), coeff_pad, source, fine_diag, omega_value)
    return pressure


def solution(mesh):
    in_specs = (P("gx", "gy", "gz"), P("gx", "gy", "gz"))
    out_specs = P("gx", "gy", "gz")
    return jax.shard_map(local, mesh=mesh, in_specs=in_specs, out_specs=out_specs, check_vma=False)
```

profile of v0, /device:TPU:1, one launch (start us, length us, event | category | flops | bytes accessed | tf_op | source)
XLA Modules:
  0.0 327.2 jit_solution(9885016076376212797)
XLA Ops:
  0.7 4.5 %collective-permute-start.1 = (f32[1,32,128]{2,1,0:T(8,128)S(1)}, f32[1,32,128]{2,1,0:T(8,128)S(1)}, u32[]{:S(2)}, u32[]{:S(2)}) collective-permute-start(f32[1,32,128]{2,1,0:T(8,128)S(1)} %get-tuple-element.54), channel_id=1, source_target_pairs={{0,8},{8,16},{16,24},{1,9},{9,17},{17,25},{2,10},{10,18},{18,26},{... | collective-permute-start | bytes 49160 | tf_op jit(solution)/shard_map/ppermute | solution.py:28
  11.6 4.0 %collective-permute-start.3 = (f32[10,1,128]{2,1,0:T(1,128)S(1)}, f32[10,1,128]{2,1,0:T(1,128)S(1)}, u32[]{:S(2)}, u32[]{:S(2)}) collective-permute-start(f32[10,1,128]{2,1,0:T(1,128)S(1)} %get-tuple-element.38), channel_id=1, source_target_pairs={{0,4},{1,5},{2,6},{3,7},{8,12},{9,13},{10,14},{11,15},{16,20},{17,... | collective-permute-start | bytes 15368 | tf_op jit(solution)/shard_map/ppermute | solution.py:28
  17.8 4.0 %collective-permute-start.5 = (f32[10,34,1]{2,1,0:T(8,128)S(1)}, f32[10,34,1]{2,1,0:T(8,128)S(1)}, u32[]{:S(2)}, u32[]{:S(2)}) collective-permute-start(f32[10,34,1]{2,1,0:T(8,128)S(1)} %get-tuple-element.26), channel_id=1, source_target_pairs={{0,1},{1,2},{2,3},{4,5},{5,6},{6,7},{8,9},{9,10},{10,11},{12,13},{... | collective-permute-start | bytes 4088 | tf_op jit(solution)/shard_map/ppermute | solution.py:28
  35.8 4.0 %collective-permute-start.9 = (f32[10,1,128]{2,1,0:T(1,128)S(1)}, f32[10,1,128]{2,1,0:T(1,128)S(1)}, u32[]{:S(2)}, u32[]{:S(2)}) collective-permute-start(f32[10,1,128]{2,1,0:T(1,128)S(1)} %get-tuple-element.36), channel_id=1, source_target_pairs={{0,4},{1,5},{2,6},{3,7},{8,12},{9,13},{10,14},{11,15},{16,20},{17,... | collective-permute-start | bytes 15368 | tf_op jit(solution)/shard_map/ppermute | solution.py:28
  57.2 4.0 %collective-permute-start.13 = (f32[1,32,128]{2,1,0:T(8,128)S(1)}, f32[1,32,128]{2,1,0:T(8,128)S(1)}, u32[]{:S(2)}, u32[]{:S(2)}) collective-permute-start(f32[1,32,128]{2,1,0:T(8,128)S(1)} %get-tuple-element.50), channel_id=1, source_target_pairs={{0,8},{8,16},{16,24},{1,9},{9,17},{17,25},{2,10},{10,18},{18,26},{... | collective-permute-start | bytes 49160 | tf_op jit(solution)/shard_map/ppermute | solution.py:28
  61.3 10.5 %reshape.34 = f32[4,2,16,2,64,2]{5,4,3,2,1,0:T(8,128)} reshape(f32[8,32,128]{2,1,0:T(8,128)} %param.3) | data formatting | bytes 262144 | tf_op jit(solution)/shard_map/reshape | solution.py:113
  71.8 4.0 %reduce_sum.18 = f32[4,16,64]{2,1,0:T(8,128)S(1)} reduce(f32[4,2,16,2,64,2]{5,4,3,2,1,0:T(8,128)} %reshape.34, f32[]{:T(128)} %constant.32.clone.1), dimensions={1,3,5}, to_apply=%region_0.0 | reduce | flops 28672 | bytes 147460 | tf_op jit(solution)/shard_map/reduce_sum | solution.py:113
  77.2 4.0 %collective-permute-start.15 = (f32[10,1,128]{2,1,0:T(1,128)S(1)}, f32[10,1,128]{2,1,0:T(1,128)S(1)}, u32[]{:S(2)}, u32[]{:S(2)}) collective-permute-start(f32[10,1,128]{2,1,0:T(1,128)S(1)} %get-tuple-element.34), channel_id=1, source_target_pairs={{0,4},{1,5},{2,6},{3,7},{8,12},{9,13},{10,14},{11,15},{16,20},{17,... | collective-permute-start | bytes 15368 | tf_op jit(solution)/shard_map/ppermute | solution.py:28
  101.1 4.0 %collective-permute-start.27 = (f32[6,1,64]{2,1,0:T(1,128)S(1)}, f32[6,1,64]{2,1,0:T(1,128)S(1)}, u32[]{:S(2)}, u32[]{:S(2)}) collective-permute-start(f32[6,1,64]{2,1,0:T(1,128)S(1)} %get-tuple-element.90), channel_id=1, source_target_pairs={{0,4},{1,5},{2,6},{3,7},{8,12},{9,13},{10,14},{11,15},{16,20},{17,... | collective-permute-start | bytes 4616 | tf_op jit(solution)/shard_map/ppermute | solution.py:28
  106.4 4.0 %collective-permute-start.20 = (f32[10,1,128]{2,1,0:T(1,128)S(1)}, f32[10,1,128]{2,1,0:T(1,128)S(1)}, u32[]{:S(2)}, u32[]{:S(2)}) collective-permute-start(f32[10,1,128]{2,1,0:T(1,128)S(1)} %get-tuple-element.32), channel_id=1, source_target_pairs={{0,4},{1,5},{2,6},{3,7},{8,12},{9,13},{10,14},{11,15},{16,20},{17,... | collective-permute-start | bytes 15368 | tf_op jit(solution)/shard_map/ppermute | solution.py:28
  112.6 4.0 %collective-permute-start.22 = (f32[10,34,1]{2,1,0:T(8,128)S(1)}, f32[10,34,1]{2,1,0:T(8,128)S(1)}, u32[]{:S(2)}, u32[]{:S(2)}) collective-permute-start(f32[10,34,1]{2,1,0:T(8,128)S(1)} %get-tuple-element.20), channel_id=1, source_target_pairs={{0,1},{1,2},{2,3},{4,5},{5,6},{6,7},{8,9},{9,10},{10,11},{12,13},{... | collective-permute-start | bytes 4088 | tf_op jit(solution)/shard_map/ppermute | solution.py:28
  118.0 4.0 %collective-permute-start.29 = (f32[6,18,1]{2,1,0:T(8,128)S(1)}, f32[6,18,1]{2,1,0:T(8,128)S(1)}, u32[]{:S(2)}, u32[]{:S(2)}) collective-permute-start(f32[6,18,1]{2,1,0:T(8,128)S(1)} %get-tuple-element.74), channel_id=1, source_target_pairs={{0,1},{1,2},{2,3},{4,5},{5,6},{6,7},{8,9},{9,10},{10,11},{12,13},{... | collective-permute-start | bytes 1304 | tf_op jit(solution)/shard_map/ppermute | solution.py:28
  125.1 4.2 %collective-permute-start.30 = (f32[1,16,64]{2,1,0:T(8,128)S(1)}, f32[1,16,64]{2,1,0:T(8,128)S(1)}, u32[]{:S(2)}, u32[]{:S(2)}) collective-permute-start(f32[1,16,64]{2,1,0:T(8,128)S(1)} %get-tuple-element.109), channel_id=1, source_target_pairs={{8,0},{16,8},{24,16},{9,1},{17,9},{25,17},{10,2},{18,10},{26,18},{... | collective-permute-start | bytes 12296 | tf_op jit(solution)/shard_map/ppermute | solution.py:30
  133.9 4.0 %collective-permute-start.33 = (f32[6,1,64]{2,1,0:T(1,128)S(1)}, f32[6,1,64]{2,1,0:T(1,128)S(1)}, u32[]{:S(2)}, u32[]{:S(2)}) collective-permute-start(f32[6,1,64]{2,1,0:T(1,128)S(1)} %get-tuple-element.88), channel_id=1, source_target_pairs={{0,4},{1,5},{2,6},{3,7},{8,12},{9,13},{10,14},{11,15},{16,20},{17,... | collective-permute-start | bytes 4616 | tf_op jit(solution)/shard_map/ppermute | solution.py:28
  147.1 4.5 %collective-permute-start.36 = (f32[1,16,64]{2,1,0:T(8,128)S(1)}, f32[1,16,64]{2,1,0:T(8,128)S(1)}, u32[]{:S(2)}, u32[]{:S(2)}) collective-permute-start(f32[1,16,64]{2,1,0:T(8,128)S(1)} %get-tuple-element.107), channel_id=1, source_target_pairs={{8,0},{16,8},{24,16},{9,1},{17,9},{25,17},{10,2},{18,10},{26,18},{... | collective-permute-start | bytes 12296 | tf_op jit(solution)/shard_map/ppermute | solution.py:30
  151.6 4.2 %collective-permute-start.37 = (f32[1,16,64]{2,1,0:T(8,128)S(1)}, f32[1,16,64]{2,1,0:T(8,128)S(1)}, u32[]{:S(2)}, u32[]{:S(2)}) collective-permute-start(f32[1,16,64]{2,1,0:T(8,128)S(1)} %get-tuple-element.106), channel_id=1, source_target_pairs={{0,8},{8,16},{16,24},{1,9},{9,17},{17,25},{2,10},{10,18},{18,26},{... | collective-permute-start | bytes 12296 | tf_op jit(solution)/shard_map/ppermute | solution.py:28
  157.9 4.0 %collective-permute-start.39 = (f32[6,1,64]{2,1,0:T(1,128)S(1)}, f32[6,1,64]{2,1,0:T(1,128)S(1)}, u32[]{:S(2)}, u32[]{:S(2)}) collective-permute-start(f32[6,1,64]{2,1,0:T(1,128)S(1)} %get-tuple-element.86), channel_id=1, source_target_pairs={{0,4},{1,5},{2,6},{3,7},{8,12},{9,13},{10,14},{11,15},{16,20},{17,... | collective-permute-start | bytes 4616 | tf_op jit(solution)/shard_map/ppermute | solution.py:28
  167.6 4.1 %collective-permute-done.40 = f32[6,18,1]{2,1,0:T(8,128)S(1)} collective-permute-done((f32[6,18,1]{2,1,0:T(8,128)S(1)}, f32[6,18,1]{2,1,0:T(8,128)S(1)}, u32[]{:S(2)}, u32[]{:S(2)}) %collective-permute-start.40) | collective-permute-done | bytes 464 | tf_op jit(solution)/shard_map/ppermute | solution.py:30
  174.3 5.3 %collective-permute-start.42 = (f32[1,16,64]{2,1,0:T(8,128)S(1)}, f32[1,16,64]{2,1,0:T(8,128)S(1)}, u32[]{:S(2)}, u32[]{:S(2)}) collective-permute-start(f32[1,16,64]{2,1,0:T(8,128)S(1)} %get-tuple-element.104), channel_id=1, source_target_pairs={{0,8},{8,16},{16,24},{1,9},{9,17},{17,25},{2,10},{10,18},{18,26},{... | collective-permute-start | bytes 12296 | tf_op jit(solution)/shard_map/ppermute | solution.py:28
  181.7 4.0 %collective-permute-start.44 = (f32[6,1,64]{2,1,0:T(1,128)S(1)}, f32[6,1,64]{2,1,0:T(1,128)S(1)}, u32[]{:S(2)}, u32[]{:S(2)}) collective-permute-start(f32[6,1,64]{2,1,0:T(1,128)S(1)} %get-tuple-element.84), channel_id=1, source_target_pairs={{0,4},{1,5},{2,6},{3,7},{8,12},{9,13},{10,14},{11,15},{16,20},{17,... | collective-permute-start | bytes 4616 | tf_op jit(solution)/shard_map/ppermute | solution.py:28
  187.8 4.0 %collective-permute-start.46 = (f32[6,18,1]{2,1,0:T(8,128)S(1)}, f32[6,18,1]{2,1,0:T(8,128)S(1)}, u32[]{:S(2)}, u32[]{:S(2)}) collective-permute-start(f32[6,18,1]{2,1,0:T(8,128)S(1)} %get-tuple-element.68), channel_id=1, source_target_pairs={{0,1},{1,2},{2,3},{4,5},{5,6},{6,7},{8,9},{9,10},{10,11},{12,13},{... | collective-permute-start | bytes 1304 | tf_op jit(solution)/shard_map/ppermute | solution.py:28
  206.3 7.0 %collective-permute-start.52 = (f32[1,16,64]{2,1,0:T(8,128)S(1)}, f32[1,16,64]{2,1,0:T(8,128)S(1)}, u32[]{:S(2)}, u32[]{:S(2)}) collective-permute-start(f32[1,16,64]{2,1,0:T(8,128)S(1)} %get-tuple-element.96), channel_id=1, source_target_pairs={{0,8},{8,16},{16,24},{1,9},{9,17},{17,25},{2,10},{10,18},{18,26},{... | collective-permute-start | bytes 12296 | tf_op jit(solution)/shard_map/ppermute | solution.py:28
  215.5 4.0 %collective-permute-start.54 = (f32[6,1,64]{2,1,0:T(1,128)S(1)}, f32[6,1,64]{2,1,0:T(1,128)S(1)}, u32[]{:S(2)}, u32[]{:S(2)}) collective-permute-start(f32[6,1,64]{2,1,0:T(1,128)S(1)} %get-tuple-element.82), channel_id=1, source_target_pairs={{0,4},{1,5},{2,6},{3,7},{8,12},{9,13},{10,14},{11,15},{16,20},{17,... | collective-permute-start | bytes 4616 | tf_op jit(solution)/shard_map/ppermute | solution.py:28
  231.1 6.8 %collective-permute-start.58 = (f32[1,16,64]{2,1,0:T(8,128)S(1)}, f32[1,16,64]{2,1,0:T(8,128)S(1)}, u32[]{:S(2)}, u32[]{:S(2)}) collective-permute-start(f32[1,16,64]{2,1,0:T(8,128)S(1)} %get-tuple-element.94), channel_id=1, source_target_pairs={{0,8},{8,16},{16,24},{1,9},{9,17},{17,25},{2,10},{10,18},{18,26},{... | collective-permute-start | bytes 12296 | tf_op jit(solution)/shard_map/ppermute | solution.py:28
  239.9 4.0 %collective-permute-start.60 = (f32[6,1,64]{2,1,0:T(1,128)S(1)}, f32[6,1,64]{2,1,0:T(1,128)S(1)}, u32[]{:S(2)}, u32[]{:S(2)}) collective-permute-start(f32[6,1,64]{2,1,0:T(1,128)S(1)} %get-tuple-element.80), channel_id=1, source_target_pairs={{0,4},{1,5},{2,6},{3,7},{8,12},{9,13},{10,14},{11,15},{16,20},{17,... | collective-permute-start | bytes 4616 | tf_op jit(solution)/shard_map/ppermute | solution.py:28
  254.6 6.8 %collective-permute-start.63 = (f32[1,16,64]{2,1,0:T(8,128)S(1)}, f32[1,16,64]{2,1,0:T(8,128)S(1)}, u32[]{:S(2)}, u32[]{:S(2)}) collective-permute-start(f32[1,16,64]{2,1,0:T(8,128)S(1)} %get-tuple-element.92), channel_id=1, source_target_pairs={{0,8},{8,16},{16,24},{1,9},{9,17},{17,25},{2,10},{10,18},{18,26},{... | collective-permute-start | bytes 12296 | tf_op jit(solution)/shard_map/ppermute | solution.py:28
  263.5 4.0 %collective-permute-start.65 = (f32[6,1,64]{2,1,0:T(1,128)S(1)}, f32[6,1,64]{2,1,0:T(1,128)S(1)}, u32[]{:S(2)}, u32[]{:S(2)}) collective-permute-start(f32[6,1,64]{2,1,0:T(1,128)S(1)} %get-tuple-element.78), channel_id=1, source_target_pairs={{0,4},{1,5},{2,6},{3,7},{8,12},{9,13},{10,14},{11,15},{16,20},{17,... | collective-permute-start | bytes 4616 | tf_op jit(solution)/shard_map/ppermute | solution.py:28
  269.6 4.0 %collective-permute-start.67 = (f32[6,18,1]{2,1,0:T(8,128)S(1)}, f32[6,18,1]{2,1,0:T(8,128)S(1)}, u32[]{:S(2)}, u32[]{:S(2)}) collective-permute-start(f32[6,18,1]{2,1,0:T(8,128)S(1)} %get-tuple-element.60), channel_id=1, source_target_pairs={{0,1},{1,2},{2,3},{4,5},{5,6},{6,7},{8,9},{9,10},{10,11},{12,13},{... | collective-permute-start | bytes 1304 | tf_op jit(solution)/shard_map/ppermute | solution.py:28
  277.9 6.5 %collective-permute-start.70 = (f32[1,32,128]{2,1,0:T(8,128)S(1)}, f32[1,32,128]{2,1,0:T(8,128)S(1)}, u32[]{:S(2)}, u32[]{:S(2)}) collective-permute-start(f32[1,32,128]{2,1,0:T(8,128)S(1)} %get-tuple-element.42), channel_id=1, source_target_pairs={{0,8},{8,16},{16,24},{1,9},{9,17},{17,25},{2,10},{10,18},{18,26},{... | collective-permute-start | bytes 49160 | tf_op jit(solution)/shard_map/ppermute | solution.py:28
  286.5 4.0 %collective-permute-start.72 = (f32[10,1,128]{2,1,0:T(1,128)S(1)}, f32[10,1,128]{2,1,0:T(1,128)S(1)}, u32[]{:S(2)}, u32[]{:S(2)}) collective-permute-start(f32[10,1,128]{2,1,0:T(1,128)S(1)} %get-tuple-element.30), channel_id=1, source_target_pairs={{0,4},{1,5},{2,6},{3,7},{8,12},{9,13},{10,14},{11,15},{16,20},{17,... | collective-permute-start | bytes 15368 | tf_op jit(solution)/shard_map/ppermute | solution.py:28
  291.4 4.0 %collective-permute-start.74 = (f32[10,34,1]{2,1,0:T(8,128)S(1)}, f32[10,34,1]{2,1,0:T(8,128)S(1)}, u32[]{:S(2)}, u32[]{:S(2)}) collective-permute-start(f32[10,34,1]{2,1,0:T(8,128)S(1)} %get-tuple-element.19), channel_id=1, source_target_pairs={{0,1},{1,2},{2,3},{4,5},{5,6},{6,7},{8,9},{9,10},{10,11},{12,13},{... | collective-permute-start | bytes 4088 | tf_op jit(solution)/shard_map/ppermute | solution.py:28
  304.1 6.8 %collective-permute-start.76 = (f32[1,32,128]{2,1,0:T(8,128)S(1)}, f32[1,32,128]{2,1,0:T(8,128)S(1)}, u32[]{:S(2)}, u32[]{:S(2)}) collective-permute-start(f32[1,32,128]{2,1,0:T(8,128)S(1)} %get-tuple-element.40), channel_id=1, source_target_pairs={{0,8},{8,16},{16,24},{1,9},{9,17},{17,25},{2,10},{10,18},{18,26},{... | collective-permute-start | bytes 49160 | tf_op jit(solution)/shard_map/ppermute | solution.py:28
  (260 shorter events, 174.7 us)
Async XLA Ops:
  16.5 8.3 %collective-permute-start.4 = (f32[10,34,1]{2,1,0:T(8,128)S(1)}, f32[10,34,1]{2,1,0:T(8,128)S(1)}, u32[]{:S(2)}, u32[]{:S(2)}) collective-permute-start(f32[10,34,1]{2,1,0:T(8,128)S(1)} %get-tuple-element.27), channel_id=1, source_target_pairs={{1,0},{2,1},{3,2},{5,4},{6,5},{7,6},{9,8},{10,9},{11,10},{13,12},{... | collective-permute-start | bytes 4088 | tf_op jit(solution)/shard_map/ppermute | solution.py:30
  17.8 8.9 %collective-permute-start.5 = (f32[10,34,1]{2,1,0:T(8,128)S(1)}, f32[10,34,1]{2,1,0:T(8,128)S(1)}, u32[]{:S(2)}, u32[]{:S(2)}) collective-permute-start(f32[10,34,1]{2,1,0:T(8,128)S(1)} %get-tuple-element.26), channel_id=1, source_target_pairs={{0,1},{1,2},{2,3},{4,5},{5,6},{6,7},{8,9},{9,10},{10,11},{12,13},{... | collective-permute-start | bytes 4088 | tf_op jit(solution)/shard_map/ppermute | solution.py:28
  40.6 8.1 %collective-permute-start.11 = (f32[10,34,1]{2,1,0:T(8,128)S(1)}, f32[10,34,1]{2,1,0:T(8,128)S(1)}, u32[]{:S(2)}, u32[]{:S(2)}) collective-permute-start(f32[10,34,1]{2,1,0:T(8,128)S(1)} %get-tuple-element.25), channel_id=1, source_target_pairs={{0,1},{1,2},{2,3},{4,5},{5,6},{6,7},{8,9},{9,10},{10,11},{12,13},{... | collective-permute-start | bytes 4088 | tf_op jit(solution)/shard_map/ppermute | solution.py:28
  44.6 8.0 %collective-permute-start.10 = (f32[10,34,1]{2,1,0:T(8,128)S(1)}, f32[10,34,1]{2,1,0:T(8,128)S(1)}, u32[]{:S(2)}, u32[]{:S(2)}) collective-permute-start(f32[10,34,1]{2,1,0:T(8,128)S(1)} %get-tuple-element.24), channel_id=1, source_target_pairs={{1,0},{2,1},{3,2},{5,4},{6,5},{7,6},{9,8},{10,9},{11,10},{13,12},{... | collective-permute-start | bytes 4088 | tf_op jit(solution)/shard_map/ppermute | solution.py:30
  53.9 21.9 %collective-permute-start.12 = (f32[1,32,128]{2,1,0:T(8,128)S(1)}, f32[1,32,128]{2,1,0:T(8,128)S(1)}, u32[]{:S(2)}, u32[]{:S(2)}) collective-permute-start(f32[1,32,128]{2,1,0:T(8,128)S(1)} %get-tuple-element.51), channel_id=1, source_target_pairs={{8,0},{16,8},{24,16},{9,1},{17,9},{25,17},{10,2},{18,10},{26,18},{... | collective-permute-start | bytes 49160 | tf_op jit(solution)/shard_map/ppermute | solution.py:30
  57.2 18.6 %collective-permute-start.13 = (f32[1,32,128]{2,1,0:T(8,128)S(1)}, f32[1,32,128]{2,1,0:T(8,128)S(1)}, u32[]{:S(2)}, u32[]{:S(2)}) collective-permute-start(f32[1,32,128]{2,1,0:T(8,128)S(1)} %get-tuple-element.50), channel_id=1, source_target_pairs={{0,8},{8,16},{16,24},{1,9},{9,17},{17,25},{2,10},{10,18},{18,26},{... | collective-permute-start | bytes 49160 | tf_op jit(solution)/shard_map/ppermute | solution.py:28
  82.1 10.3 %collective-permute-start.17 = (f32[10,34,1]{2,1,0:T(8,128)S(1)}, f32[10,34,1]{2,1,0:T(8,128)S(1)}, u32[]{:S(2)}, u32[]{:S(2)}) collective-permute-start(f32[10,34,1]{2,1,0:T(8,128)S(1)} %get-tuple-element.23), channel_id=1, source_target_pairs={{0,1},{1,2},{2,3},{4,5},{5,6},{6,7},{8,9},{9,10},{10,11},{12,13},{... | collective-permute-start | bytes 4088 | tf_op jit(solution)/shard_map/ppermute | solution.py:28
  85.3 8.7 %collective-permute-start.16 = (f32[10,34,1]{2,1,0:T(8,128)S(1)}, f32[10,34,1]{2,1,0:T(8,128)S(1)}, u32[]{:S(2)}, u32[]{:S(2)}) collective-permute-start(f32[10,34,1]{2,1,0:T(8,128)S(1)} %get-tuple-element.22), channel_id=1, source_target_pairs={{1,0},{2,1},{3,2},{5,4},{6,5},{7,6},{9,8},{10,9},{11,10},{13,12},{... | collective-permute-start | bytes 4088 | tf_op jit(solution)/shard_map/ppermute | solution.py:30
  86.6 13.2 %collective-permute-start.24 = (f32[1,16,64]{2,1,0:T(8,128)S(1)}, f32[1,16,64]{2,1,0:T(8,128)S(1)}, u32[]{:S(2)}, u32[]{:S(2)}) collective-permute-start(f32[1,16,64]{2,1,0:T(8,128)S(1)} %get-tuple-element.111), channel_id=1, source_target_pairs={{8,0},{16,8},{24,16},{9,1},{17,9},{25,17},{10,2},{18,10},{26,18},{... | collective-permute-start | bytes 12296 | tf_op jit(solution)/shard_map/ppermute | solution.py:30
  88.5 11.3 %collective-permute-start.25 = (f32[1,16,64]{2,1,0:T(8,128)S(1)}, f32[1,16,64]{2,1,0:T(8,128)S(1)}, u32[]{:S(2)}, u32[]{:S(2)}) collective-permute-start(f32[1,16,64]{2,1,0:T(8,128)S(1)} %get-tuple-element.110), channel_id=1, source_target_pairs={{0,8},{8,16},{16,24},{1,9},{9,17},{17,25},{2,10},{10,18},{18,26},{... | collective-permute-start | bytes 12296 | tf_op jit(solution)/shard_map/ppermute | solution.py:28
  94.2 10.9 %collective-permute-start.19 = (f32[1,32,128]{2,1,0:T(8,128)S(1)}, f32[1,32,128]{2,1,0:T(8,128)S(1)}, u32[]{:S(2)}, u32[]{:S(2)}) collective-permute-start(f32[1,32,128]{2,1,0:T(8,128)S(1)} %get-tuple-element.49), channel_id=1, source_target_pairs={{8,0},{16,8},{24,16},{9,1},{17,9},{25,17},{10,2},{18,10},{26,18},{... | collective-permute-start | bytes 49160 | tf_op jit(solution)/shard_map/ppermute | solution.py:30
  96.8 8.3 %collective-permute-start.18 = (f32[1,32,128]{2,1,0:T(8,128)S(1)}, f32[1,32,128]{2,1,0:T(8,128)S(1)}, u32[]{:S(2)}, u32[]{:S(2)}) collective-permute-start(f32[1,32,128]{2,1,0:T(8,128)S(1)} %get-tuple-element.48), channel_id=1, source_target_pairs={{0,8},{8,16},{16,24},{1,9},{9,17},{17,25},{2,10},{10,18},{18,26},{... | collective-permute-start | bytes 49160 | tf_op jit(solution)/shard_map/ppermute | solution.py:28
  99.8 10.6 %collective-permute-start.26 = (f32[6,1,64]{2,1,0:T(1,128)S(1)}, f32[6,1,64]{2,1,0:T(1,128)S(1)}, u32[]{:S(2)}, u32[]{:S(2)}) collective-permute-start(f32[6,1,64]{2,1,0:T(1,128)S(1)} %get-tuple-element.91), channel_id=1, source_target_pairs={{4,0},{5,1},{6,2},{7,3},{12,8},{13,9},{14,10},{15,11},{20,16},{21,... | collective-permute-start | bytes 4616 | tf_op jit(solution)/shard_map/ppermute | solution.py:30
  101.1 9.3 %collective-permute-start.27 = (f32[6,1,64]{2,1,0:T(1,128)S(1)}, f32[6,1,64]{2,1,0:T(1,128)S(1)}, u32[]{:S(2)}, u32[]{:S(2)}) collective-permute-start(f32[6,1,64]{2,1,0:T(1,128)S(1)} %get-tuple-element.90), channel_id=1, source_target_pairs={{0,4},{1,5},{2,6},{3,7},{8,12},{9,13},{10,14},{11,15},{16,20},{17,... | collective-permute-start | bytes 4616 | tf_op jit(solution)/shard_map/ppermute | solution.py:28
  111.3 10.7 %collective-permute-start.23 = (f32[10,34,1]{2,1,0:T(8,128)S(1)}, f32[10,34,1]{2,1,0:T(8,128)S(1)}, u32[]{:S(2)}, u32[]{:S(2)}) collective-permute-start(f32[10,34,1]{2,1,0:T(8,128)S(1)} %get-tuple-element.21), channel_id=1, source_target_pairs={{1,0},{2,1},{3,2},{5,4},{6,5},{7,6},{9,8},{10,9},{11,10},{13,12},{... | collective-permute-start | bytes 4088 | tf_op jit(solution)/shard_map/ppermute | solution.py:30
  112.6 9.4 %collective-permute-start.22 = (f32[10,34,1]{2,1,0:T(8,128)S(1)}, f32[10,34,1]{2,1,0:T(8,128)S(1)}, u32[]{:S(2)}, u32[]{:S(2)}) collective-permute-start(f32[10,34,1]{2,1,0:T(8,128)S(1)} %get-tuple-element.20), channel_id=1, source_target_pairs={{0,1},{1,2},{2,3},{4,5},{5,6},{6,7},{8,9},{9,10},{10,11},{12,13},{... | collective-permute-start | bytes 4088 | tf_op jit(solution)/shard_map/ppermute | solution.py:28
  116.7 8.3 %collective-permute-start.28 = (f32[6,18,1]{2,1,0:T(8,128)S(1)}, f32[6,18,1]{2,1,0:T(8,128)S(1)}, u32[]{:S(2)}, u32[]{:S(2)}) collective-permute-start(f32[6,18,1]{2,1,0:T(8,128)S(1)} %get-tuple-element.75), channel_id=1, source_target_pairs={{1,0},{2,1},{3,2},{5,4},{6,5},{7,6},{9,8},{10,9},{11,10},{13,12},{... | collective-permute-start | bytes 1304 | tf_op jit(solution)/shard_map/ppermute | solution.py:30
  118.0 7.0 %collective-permute-start.29 = (f32[6,18,1]{2,1,0:T(8,128)S(1)}, f32[6,18,1]{2,1,0:T(8,128)S(1)}, u32[]{:S(2)}, u32[]{:S(2)}) collective-permute-start(f32[6,18,1]{2,1,0:T(8,128)S(1)} %get-tuple-element.74), channel_id=1, source_target_pairs={{0,1},{1,2},{2,3},{4,5},{5,6},{6,7},{8,9},{9,10},{10,11},{12,13},{... | collective-permute-start | bytes 1304 | tf_op jit(solution)/shard_map/ppermute | solution.py:28
  125.1 6.7 %collective-permute-start.30 = (f32[1,16,64]{2,1,0:T(8,128)S(1)}, f32[1,16,64]{2,1,0:T(8,128)S(1)}, u32[]{:S(2)}, u32[]{:S(2)}) collective-permute-start(f32[1,16,64]{2,1,0:T(8,128)S(1)} %get-tuple-element.109), channel_id=1, source_target_pairs={{8,0},{16,8},{24,16},{9,1},{17,9},{25,17},{10,2},{18,10},{26,18},{... | collective-permute-start | bytes 12296 | tf_op jit(solution)/shard_map/ppermute | solution.py:30
  147.1 8.7 %collective-permute-start.36 = (f32[1,16,64]{2,1,0:T(8,128)S(1)}, f32[1,16,64]{2,1,0:T(8,128)S(1)}, u32[]{:S(2)}, u32[]{:S(2)}) collective-permute-start(f32[1,16,64]{2,1,0:T(8,128)S(1)} %get-tuple-element.107), channel_id=1, source_target_pairs={{8,0},{16,8},{24,16},{9,1},{17,9},{25,17},{10,2},{18,10},{26,18},{... | collective-permute-start | bytes 12296 | tf_op jit(solution)/shard_map/ppermute | solution.py:30
  171.9 7.7 %collective-permute-start.43 = (f32[1,16,64]{2,1,0:T(8,128)S(1)}, f32[1,16,64]{2,1,0:T(8,128)S(1)}, u32[]{:S(2)}, u32[]{:S(2)}) collective-permute-start(f32[1,16,64]{2,1,0:T(8,128)S(1)} %get-tuple-element.105), channel_id=1, source_target_pairs={{8,0},{16,8},{24,16},{9,1},{17,9},{25,17},{10,2},{18,10},{26,18},{... | collective-permute-start | bytes 12296 | tf_op jit(solution)/shard_map/ppermute | solution.py:30
  204.1 9.3 %collective-permute-start.51 = (f32[1,16,64]{2,1,0:T(8,128)S(1)}, f32[1,16,64]{2,1,0:T(8,128)S(1)}, u32[]{:S(2)}, u32[]{:S(2)}) collective-permute-start(f32[1,16,64]{2,1,0:T(8,128)S(1)} %get-tuple-element.97), channel_id=1, source_target_pairs={{8,0},{16,8},{24,16},{9,1},{17,9},{25,17},{10,2},{18,10},{26,18},{... | collective-permute-start | bytes 12296 | tf_op jit(solution)/shard_map/ppermute | solution.py:30
  206.3 7.8 %collective-permute-start.52 = (f32[1,16,64]{2,1,0:T(8,128)S(1)}, f32[1,16,64]{2,1,0:T(8,128)S(1)}, u32[]{:S(2)}, u32[]{:S(2)}) collective-permute-start(f32[1,16,64]{2,1,0:T(8,128)S(1)} %get-tuple-element.96), channel_id=1, source_target_pairs={{0,8},{8,16},{16,24},{1,9},{9,17},{17,25},{2,10},{10,18},{18,26},{... | collective-permute-start | bytes 12296 | tf_op jit(solution)/shard_map/ppermute | solution.py:28
  229.1 8.7 %collective-permute-start.57 = (f32[1,16,64]{2,1,0:T(8,128)S(1)}, f32[1,16,64]{2,1,0:T(8,128)S(1)}, u32[]{:S(2)}, u32[]{:S(2)}) collective-permute-start(f32[1,16,64]{2,1,0:T(8,128)S(1)} %get-tuple-element.95), channel_id=1, source_target_pairs={{8,0},{16,8},{24,16},{9,1},{17,9},{25,17},{10,2},{18,10},{26,18},{... | collective-permute-start | bytes 12296 | tf_op jit(solution)/shard_map/ppermute | solution.py:30
  231.1 7.5 %collective-permute-start.58 = (f32[1,16,64]{2,1,0:T(8,128)S(1)}, f32[1,16,64]{2,1,0:T(8,128)S(1)}, u32[]{:S(2)}, u32[]{:S(2)}) collective-permute-start(f32[1,16,64]{2,1,0:T(8,128)S(1)} %get-tuple-element.94), channel_id=1, source_target_pairs={{0,8},{8,16},{16,24},{1,9},{9,17},{17,25},{2,10},{10,18},{18,26},{... | collective-permute-start | bytes 12296 | tf_op jit(solution)/shard_map/ppermute | solution.py:28
  252.7 8.7 %collective-permute-start.64 = (f32[1,16,64]{2,1,0:T(8,128)S(1)}, f32[1,16,64]{2,1,0:T(8,128)S(1)}, u32[]{:S(2)}, u32[]{:S(2)}) collective-permute-start(f32[1,16,64]{2,1,0:T(8,128)S(1)} %get-tuple-element.93), channel_id=1, source_target_pairs={{8,0},{16,8},{24,16},{9,1},{17,9},{25,17},{10,2},{18,10},{26,18},{... | collective-permute-start | bytes 12296 | tf_op jit(solution)/shard_map/ppermute | solution.py:30
  254.6 7.5 %collective-permute-start.63 = (f32[1,16,64]{2,1,0:T(8,128)S(1)}, f32[1,16,64]{2,1,0:T(8,128)S(1)}, u32[]{:S(2)}, u32[]{:S(2)}) collective-permute-start(f32[1,16,64]{2,1,0:T(8,128)S(1)} %get-tuple-element.92), channel_id=1, source_target_pairs={{0,8},{8,16},{16,24},{1,9},{9,17},{17,25},{2,10},{10,18},{18,26},{... | collective-permute-start | bytes 12296 | tf_op jit(solution)/shard_map/ppermute | solution.py:28
  276.0 8.4 %collective-permute-start.69 = (f32[1,32,128]{2,1,0:T(8,128)S(1)}, f32[1,32,128]{2,1,0:T(8,128)S(1)}, u32[]{:S(2)}, u32[]{:S(2)}) collective-permute-start(f32[1,32,128]{2,1,0:T(8,128)S(1)} %get-tuple-element.43), channel_id=1, source_target_pairs={{8,0},{16,8},{24,16},{9,1},{17,9},{25,17},{10,2},{18,10},{26,18},{... | collective-permute-start | bytes 49160 | tf_op jit(solution)/shard_map/ppermute | solution.py:30
  277.9 7.3 %collective-permute-start.70 = (f32[1,32,128]{2,1,0:T(8,128)S(1)}, f32[1,32,128]{2,1,0:T(8,128)S(1)}, u32[]{:S(2)}, u32[]{:S(2)}) collective-permute-start(f32[1,32,128]{2,1,0:T(8,128)S(1)} %get-tuple-element.42), channel_id=1, source_target_pairs={{0,8},{8,16},{16,24},{1,9},{9,17},{17,25},{2,10},{10,18},{18,26},{... | collective-permute-start | bytes 49160 | tf_op jit(solution)/shard_map/ppermute | solution.py:28
  291.4 6.7 %collective-permute-start.74 = (f32[10,34,1]{2,1,0:T(8,128)S(1)}, f32[10,34,1]{2,1,0:T(8,128)S(1)}, u32[]{:S(2)}, u32[]{:S(2)}) collective-permute-start(f32[10,34,1]{2,1,0:T(8,128)S(1)} %get-tuple-element.19), channel_id=1, source_target_pairs={{0,1},{1,2},{2,3},{4,5},{5,6},{6,7},{8,9},{9,10},{10,11},{12,13},{... | collective-permute-start | bytes 4088 | tf_op jit(solution)/shard_map/ppermute | solution.py:28
  302.2 8.7 %collective-permute-start.75 = (f32[1,32,128]{2,1,0:T(8,128)S(1)}, f32[1,32,128]{2,1,0:T(8,128)S(1)}, u32[]{:S(2)}, u32[]{:S(2)}) collective-permute-start(f32[1,32,128]{2,1,0:T(8,128)S(1)} %get-tuple-element.41), channel_id=1, source_target_pairs={{8,0},{16,8},{24,16},{9,1},{17,9},{25,17},{10,2},{18,10},{26,18},{... | collective-permute-start | bytes 49160 | tf_op jit(solution)/shard_map/ppermute | solution.py:30
  304.1 7.6 %collective-permute-start.76 = (f32[1,32,128]{2,1,0:T(8,128)S(1)}, f32[1,32,128]{2,1,0:T(8,128)S(1)}, u32[]{:S(2)}, u32[]{:S(2)}) collective-permute-start(f32[1,32,128]{2,1,0:T(8,128)S(1)} %get-tuple-element.40), channel_id=1, source_target_pairs={{0,8},{8,16},{16,24},{1,9},{9,17},{17,25},{2,10},{10,18},{18,26},{... | collective-permute-start | bytes 49160 | tf_op jit(solution)/shard_map/ppermute | solution.py:28
  (51 other events, 318.2 us)
where the time goes:
time: 332 us; the launch traced here: 327 us
  starting transfers between devices  233 us (70%)
  waiting for transfers between devices  62.7 us (19%)
  local copies, waits for them, and re-layouts  18.9 us (6%)
  other arithmetic  10.7 us (3%)
    ppermute x39, starting transfers between devices, padded_2(): lax.ppermute(tail, axis, [(i, (i + 1) % count) for i in range(ends)])  162 us
    ppermute x39, starting transfers between devices, padded_2(): lax.ppermute(head, axis, [((i + 1) % count, i) for i in range(ends)])  66.4 us
    ppermute x39, waiting for transfers between devices, padded_2(): lax.ppermute(head, axis, [((i + 1) % count, i) for i in range(ends)])  33.6 us
    ppermute x39, waiting for transfers between devices, padded_2(): lax.ppermute(tail, axis, [(i, (i + 1) % count) for i in range(ends)])  25.6 us
    reshape x1, local copies, waits for them, and re-layouts, coarsen(): values.reshape(first // 2, 2, second // 2, 2, third // 2, 2)  10.5 us
  transfers between devices with their start and end apart: 81, of which 44 were waited for; matrix products, arithmetic and copies ran while one was open for 6% of the time, Pallas kernels for 0%

commit v1 on v0

v1 whole, which is shorter than its diff:
```python
import functools
import math

import jax
import jax.numpy as jnp
from jax import lax
from jax.experimental import pallas as pl
from jax.experimental.pallas import tpu as pltpu
from jax.sharding import PartitionSpec as P

spectrum_top = 1.9
spectrum_low = 0.475
omega_first = 1.0 / (
    (spectrum_top + spectrum_low) / 2 + (spectrum_top - spectrum_low) / 2 * math.cos(math.pi / 4)
)
omega_second = 1.0 / (
    (spectrum_top + spectrum_low) / 2
    + (spectrum_top - spectrum_low) / 2 * math.cos(3 * math.pi / 4)
)
F32 = jnp.float32
MESH = pl.DeviceIdType.MESH
H = 4
T = 8
copies = 40


def iota(shape, dim):
    return lax.broadcasted_iota(jnp.int32, shape, dim)


def dot(a, b):
    return jnp.dot(a, b, precision=lax.Precision.HIGHEST, preferred_element_type=F32)


def ring(index, size, cut):
    return jnp.where(index >= cut, index - size, index)


def restrict_weight(diff):
    side = (diff == -1) | (diff == 2)
    centre = (diff == 0) | (diff == 1)
    return jnp.where(centre, 0.375, jnp.where(side, 0.125, 0.0)).astype(F32)


def mean_weight(diff):
    return jnp.where((diff == 0) | (diff == 1), 0.5, 0.0).astype(F32)


def interpolate_weight(fine, coarse):
    base = (fine + 64) // 2 - 32
    other = base + jnp.where((fine + 64) % 2 == 0, -1, 1)
    return jnp.where(coarse == base, 0.75, jnp.where(coarse == other, 0.25, 0.0)).astype(F32)


def shift(values, axis, amount):
    size = values.shape[axis]
    return pltpu.roll(values, (-amount) % size, axis)


def kernel(
    sizes, s_ref, k_ref, out_ref,
    ks, pk, pa, pb, qe, wx, wy, wz, iv, ua, ub,
    own, ma, mb, mid, cz, cg, send_sem, recv_sem,
):
    cx, cy, cz_ = s_ref.shape
    hx, hy, hz = cx // 2, cy // 2, cz_ // 2
    qx, qy, qz = cx // 4, cy // 4, cz_ // 4
    ex, ey, ez = ks.shape[1:]
    mx, my, mz = mid.shape[1:]
    pos = {axis: lax.axis_index(axis) for axis in sizes}
    used = [0]

    def make(axis, way, src, dst, number):
        return pltpu.make_async_remote_copy(
            src_ref=src, dst_ref=dst, send_sem=send_sem.at[number], recv_sem=recv_sem.at[number],
            device_id={axis: pos[axis] + way}, device_id_type=MESH,
        )

    def has(axis, way):
        return pos[axis] < sizes[axis] - 1 if way > 0 else pos[axis] > 0

    def start(items):
        started = []
        for axis, way, src, dst in items:
            number = used[0]
            used[0] += 1
            started.append((axis, way, src, dst, number))

            @pl.when(has(axis, way))
            def _():
                make(axis, way, src, dst, number).start()

        return started

    def finish(started):
        for axis, way, src, dst, number in started:

            @pl.when(has(axis, way))
            def _():
                make(axis, way, src, dst, number).wait_send()

            @pl.when(has(axis, -way))
            def _():
                make(axis, way, src, dst, number).wait_recv()

    def pair(axis, src, dst):
        number = used[0]
        used[0] += 1
        mate = pos[axis] + 1 - 2 * (pos[axis] % 2)
        return pltpu.make_async_remote_copy(
            src_ref=src, dst_ref=dst, send_sem=send_sem.at[number], recv_sem=recv_sem.at[number],
            device_id={axis: mate}, device_id_type=MESH,
        )

    def clear(i, carry):
        ks[0, i] = jnp.zeros((ey, ez), F32)
        ks[1, i] = jnp.zeros((ey, ez), F32)
        return carry

    lax.fori_loop(0, ex, clear, 0)
    qe[...] = jnp.zeros(qe.shape, F32)
    pa[...] = jnp.zeros(pa.shape, F32)
    pb[...] = jnp.zeros(pb.shape, F32)
    mid[...] = jnp.zeros(mid.shape, F32)
    ma[...] = jnp.zeros(ma.shape, F32)
    mb[...] = jnp.zeros(mb.shape, F32)
    group = iota((cy, cz_), 1) // (2 * H)
    packed = jnp.zeros((cy, cz_), F32)
    for f, ref in enumerate((k_ref, s_ref)):
        for p in range(cx):
            g = f * cx + p
            packed = jnp.where(group == g, shift(ref[p], 1, -(H + 2 * H * g)), packed)
    pk[...] = packed

    barrier = pltpu.get_barrier_semaphore()
    count = 0
    for axis in sizes:
        for way in (1, -1):
            here = has(axis, way)
            count = count + here.astype(jnp.int32)

            @pl.when(here)
            def _():
                pl.semaphore_signal(
                    barrier, inc=1, device_id={axis: pos[axis] + way}, device_id_type=MESH
                )

    pl.semaphore_wait(barrier, count)

    main = pl.ds(0, cz_)
    rows = pl.ds(T, cy)
    items = [
        ("gz", 1, pk, pa),
        ("gz", -1, pk, pb),
    ]
    for f, ref in enumerate((k_ref, s_ref)):
        items += [
            ("gx", 1, ref.at[pl.ds(cx - H, H)], ks.at[f, pl.ds(0, H), rows, main]),
            ("gx", -1, ref.at[pl.ds(0, H)], ks.at[f, pl.ds(H + cx, H), rows, main]),
            ("gy", 1, ref.at[:, pl.ds(cy - T, T)], ks.at[f, pl.ds(H, cx), pl.ds(0, T), main]),
            ("gy", -1, ref.at[:, pl.ds(0, T)], ks.at[f, pl.ds(H, cx), pl.ds(T + cy, T), main]),
        ]
    first = start(items)
    for p in range(cx):
        ks[0, H + p, T : T + cy, 0:cz_] = k_ref[p]
        ks[1, H + p, T : T + cy, 0:cz_] = s_ref[p]
    finish(first[:2])
    lane = iota((cy, cz_), 1)
    qe[1, T : T + cy, :] = jnp.where(lane % (2 * H) < H, pa[...], pb[...])
    second = start([
        ("gx", 1, qe.at[1, rows], qe.at[0, rows]),
        ("gx", -1, qe.at[1, rows], qe.at[2, rows]),
    ])
    finish(first[2:])
    items = []
    for low in (0, H + cx):
        planes = pl.ds(low, H)
        items += [
            ("gy", 1, ks.at[:, planes, pl.ds(cy, T), main], ks.at[:, planes, pl.ds(0, T), main]),
            ("gy", -1, ks.at[:, planes, pl.ds(T, T), main], ks.at[:, planes, pl.ds(T + cy, T), main]),
        ]
    third = start(items)
    finish(second)
    fourth = start([
        ("gy", 1, qe.at[:, pl.ds(cy, T)], qe.at[:, pl.ds(0, T)]),
        ("gy", -1, qe.at[:, pl.ds(T, T)], qe.at[:, pl.ds(T + cy, T)]),
    ])
    finish(third)
    finish(fourth)
    for i in range(ex):
        block, p = (i - H) // cx + 1, (i - H) % cx
        for f in range(2):
            ks[f, i, :, cz_:ez] = shift(qe[block], 1, H + 2 * H * (f * cx + p))

    r = iota((ey, ez), 0) - T + pos["gy"] * cy
    local_z = ring(iota((ey, ez), 1), ez, ez - cz_ // 2)
    z = local_z + pos["gz"] * cz_
    fine_in = (r >= 0) & (r < cy * sizes["gy"]) & (z >= 0) & (z < cz_ * sizes["gz"])
    fine_in = fine_in & (local_z >= -H) & (local_z < cz_ + H)

    def plane_in(i):
        x = i - H + pos["gx"] * cx
        return (x >= 0) & (x < cx * sizes["gx"])

    wx[0] = 0.5 * (ks[0, 0] + ks[0, 1])

    def weights(i, carry):
        k = ks[0, i]
        after = 0.5 * (k + ks[0, i + 1])
        a = 0.5 * (k + shift(k, 0, 1))
        b = 0.5 * (k + shift(k, 1, 1))
        diag = (wx[i - 1] + after) + (a + shift(a, 0, -1)) + (b + shift(b, 1, -1))
        wx[i] = after
        wy[i] = a
        wz[i] = b
        inverse = jnp.where(fine_in & plane_in(i), 1.0 / diag, 0.0)
        iv[i] = inverse
        ua[i] = omega_first * ks[1, i] * inverse
        return carry

    lax.fori_loop(1, ex - 1, weights, 0)

    def around(u, i):
        v = u[i]
        a, b = wy[i], wz[i]
        total = wx[i] * u[i + 1] + wx[i - 1] * u[i - 1]
        total = total + (a * shift(v, 0, 1) + shift(a * v, 0, -1))
        total = total + (b * shift(v, 1, 1) + shift(b * v, 1, -1))
        return v, total

    def fine_sweep(u, i, omega):
        v, total = around(u, i)
        return (1.0 - omega) * v + omega * (ks[1, i] + total) * iv[i]

    def pre(i, carry):
        ub[i] = fine_sweep(ua, i, omega_second)
        return carry

    lax.fori_loop(2, ex - 2, pre, 0)

    def leftover(i, carry):
        v, total = around(ub, i)
        inverse = iv[i]
        diag = wx[i] + wx[i - 1] + (wy[i] + shift(wy[i], 0, -1)) + (wz[i] + shift(wz[i], 1, -1))
        ua[i] = jnp.where(inverse > 0.0, ks[1, i] - diag * v + total, 0.0)
        return carry

    lax.fori_loop(3, ex - 3, leftover, 0)

    lz = ring(iota((ez, mz), 0), ez, ez - cz_ // 2) - 2 * iota((ez, mz), 1)
    keep = iota((ez, mz), 1) < hz
    to_middle_z = jnp.where(keep, restrict_weight(lz), 0.0)
    mean_z = jnp.where(keep, mean_weight(lz), 0.0)
    ly = iota((hy, ey), 1) - T - 2 * iota((hy, ey), 0)
    to_middle_y, mean_y = restrict_weight(ly), mean_weight(ly)
    combined = []
    for i in range(hx):
        c = H + 2 * i
        combined.append((ua[c - 1] + ua[c + 2]) * 0.5 + (ua[c] + ua[c + 1]) * 1.5)
    stacked = dot(jnp.concatenate(combined, axis=0), to_middle_z)
    means = [(ks[0, H + 2 * i] + ks[0, H + 2 * i + 1]) * 0.5 for i in range(hx)]
    mean_stacked = dot(jnp.concatenate(means, axis=0), mean_z)
    for i in range(hx):
        own[0, i] = dot(mean_y, mean_stacked[i * ey : (i + 1) * ey])
        own[1, i] = dot(to_middle_y, stacked[i * ey : (i + 1) * ey])

    mrows = pl.ds(T, hy)
    mlane = iota((hy, mz), 1)

    def middle_exchange(fields, put):
        inside = pl.ds(fields[0], len(fields))
        step = start([
            ("gz", 1, own.at[inside], ma.at[inside]),
            ("gz", -1, own.at[inside], mb.at[inside]),
        ])
        finish(step)
        for f in fields:
            for i in range(hx):
                side = jnp.where(mlane < (mz - hz) // 2, mb[f, i], ma[f, i])
                put(f, i, jnp.where(mlane < hz, own[f, i], shift(side, 1, hz)))
        step = start([
            ("gx", 1, mid.at[inside, pl.ds(hx, hx), mrows], mid.at[inside, pl.ds(0, hx), mrows]),
            ("gx", -1, mid.at[inside, pl.ds(hx, hx), mrows], mid.at[inside, pl.ds(2 * hx, hx), mrows]),
        ])
        finish(step)
        step = start([
            ("gy", 1, mid.at[inside, :, pl.ds(hy, T)], mid.at[inside, :, pl.ds(0, T)]),
            ("gy", -1, mid.at[inside, :, pl.ds(T, T)], mid.at[inside, :, pl.ds(T + hy, T)]),
        ])
        finish(step)

    def put(f, i, values):
        mid[f, hx + i, T : T + hy, :] = values

    middle_exchange((0, 1), put)

    mr = iota((mx, my, mz), 1) - T + pos["gy"] * hy
    mlz = ring(iota((mx, my, mz), 2), mz, (hz + mz) // 2)
    mzz = mlz + pos["gz"] * hz
    mxx = iota((mx, my, mz), 0) - hx + pos["gx"] * hx
    middle_in = (
        (mr >= 0) & (mr < hy * sizes["gy"]) & (mzz >= 0) & (mzz < hz * sizes["gz"])
        & (mxx >= 0) & (mxx < hx * sizes["gx"]) & (mlz >= -H) & (mlz < hz + H)
    )

    def up(values):
        return jnp.concatenate([values[1:], values[:1]], axis=0)

    def down(values):
        return jnp.concatenate([values[-1:], values[:-1]], axis=0)

    def faces(k):
        return 0.5 * (k + up(k)), 0.5 * (k + shift(k, 1, 1)), 0.5 * (k + shift(k, 2, 1))

    def diagonal(w):
        return (w[0] + down(w[0])) + (w[1] + shift(w[1], 1, -1)) + (w[2] + shift(w[2], 2, -1))

    def neighbours(w, v):
        total = w[0] * up(v) + down(w[0] * v)
        total = total + (w[1] * shift(v, 1, 1) + shift(w[1] * v, 1, -1))
        return total + (w[2] * shift(v, 2, 1) + shift(w[2] * v, 2, -1))

    def sweep(w, inverse, v, f, omega):
        return (1.0 - omega) * v + omega * (f + neighbours(w, v)) * inverse

    mk, mf = mid[0], mid[1]
    mw = faces(mk)
    mdiag = diagonal(mw)
    miv = jnp.where(middle_in, 1.0 / mdiag, 0.0)
    m1 = omega_first * mf * miv
    m2 = sweep(mw, miv, m1, mf, omega_second)
    mleft = jnp.where(middle_in, mf - mdiag * m2 + neighbours(mw, m2), 0.0)

    px, py, pz = pos["gx"] % 2, pos["gy"] % 2, pos["gz"] % 2
    cj = iota((mz, mz), 1) - pz * qz
    clz = ring(iota((mz, mz), 0), mz, (hz + mz) // 2) - 2 * cj
    ckeep = (cj >= 0) & (cj < qz)
    to_coarse_z = jnp.where(ckeep, restrict_weight(clz), 0.0)
    cmean_z = jnp.where(ckeep, mean_weight(clz), 0.0)
    cly = iota((qy, my), 1) - T - 2 * iota((qy, my), 0)
    to_coarse_y, cmean_y = restrict_weight(cly), mean_weight(cly)
    for i in range(qx):
        c = hx + 2 * i
        mixed = (mleft[c - 1] + mleft[c + 2]) * 0.5 + (mleft[c] + mleft[c + 1]) * 1.5
        mean = (mk[c] + mk[c + 1]) * 0.5
        cz[0, 0, i] = dot(cmean_y, dot(mean, cmean_z))
        cz[0, 1, i] = dot(to_coarse_y, dot(mixed, to_coarse_z))
    copy = pair("gz", cz.at[0], cz.at[1])
    copy.start()
    copy.wait()
    here = pl.ds(px * qx, qx)
    line = pl.ds(pl.multiple_of(py * qy, qy), qy)
    cg[:, here, line, :] = cz[0] + cz[1]
    copy = pair("gy", cg.at[:, here, line], cg.at[:, here, line])
    copy.start()
    copy.wait()
    copy = pair("gx", cg.at[:, here], cg.at[:, here])
    copy.start()
    copy.wait()

    ck, cf = cg[0], cg[1]
    cshape = ck.shape
    row = iota(cshape, 1)
    plane = iota(cshape, 0)
    box_in = iota(cshape, 2) < 2 * qz
    cw = faces(ck)
    nx, ny = 2 * qx, 2 * qy
    half = 0.5 * ck
    cwx = jnp.where(plane < nx - 1, cw[0], 0.0)
    cwy = jnp.where(row < ny - 1, cw[1], 0.0)
    cw = (cwx, cwy, cw[2])
    cdiag = diagonal(cw)
    cdiag = cdiag + jnp.where(plane == 0, half, 0.0) + jnp.where(plane == nx - 1, half, 0.0)
    cdiag = cdiag + jnp.where(row == 0, half, 0.0) + jnp.where(row == ny - 1, half, 0.0)
    civ = jnp.where(box_in, 1.0 / cdiag, 0.0)
    c1 = omega_first * cf * civ
    c2 = sweep(cw, civ, c1, cf, omega_second)
    flat = c2.reshape(nx * ny, mz)
    jj = iota((mz, mz), 1)
    back_z = interpolate_weight(jj + pz * hz, iota((mz, mz), 0))
    back_z = jnp.where((jj < hz) & (iota((mz, mz), 0) < 2 * qz), back_z, 0.0)
    shape = (hx * hy, nx * ny)
    fine_i, coarse_i = iota(shape, 0), iota(shape, 1)
    back_xy = interpolate_weight(fine_i // hy + px * hx, coarse_i // ny) * interpolate_weight(
        fine_i % hy + py * hy, coarse_i % ny
    )
    correction = dot(back_xy, dot(flat, back_z))
    for i in range(hx):
        own[2, i] = m2[hx + i, T : T + hy, :] + correction[i * hy : (i + 1) * hy]
    middle_exchange((2,), put)
    m3 = mid[2]
    m4 = sweep(mw, miv, m3, mf, omega_first)
    m5 = sweep(mw, miv, m4, mf, omega_second)

    fine_lane = ring(iota((mz, ez), 1), ez, ez - cz_ // 2)
    middle_lane = ring(iota((mz, ez), 0), mz, (hz + mz) // 2)
    wide = (fine_lane >= -H) & (fine_lane < cz_ + H)
    to_fine_z = jnp.where(wide, interpolate_weight(fine_lane, middle_lane), 0.0)
    to_fine_y = interpolate_weight(iota((ey, my), 0) - T, iota((ey, my), 1) - T)
    mixed = []
    for i in range(2, ex - 2):
        c = (i - H + 64) // 2 - 32 + hx
        other = c - 1 if i % 2 == 0 else c + 1
        mixed.append(0.75 * m5[c] + 0.25 * m5[other])
    spread = dot(jnp.concatenate(mixed, axis=0), to_fine_z)
    for i in range(2, ex - 2):
        piece = spread[(i - 2) * my : (i - 1) * my]
        fresh = dot(to_fine_y, piece)
        ua[i] = jnp.where(fine_in & plane_in(i), ub[i] + fresh, 0.0)

    def post(i, carry):
        ub[i] = fine_sweep(ua, i, omega_first)
        return carry

    lax.fori_loop(3, ex - 3, post, 0)

    def last(i, carry):
        out_ref[i - H] = fine_sweep(ub, i, omega_second)[T : T + cy, 0:cz_]
        return carry

    lax.fori_loop(H, H + cx, last, 0)


def solution(mesh):
    sizes = {axis: mesh.shape[axis] for axis in mesh.axis_names}
    spec = P("gx", "gy", "gz")

    def local(source, conductivity):
        cx, cy, cz = source.shape
        fine = (cx + 2 * H, cy + 2 * T, 2 * cz)
        mid = (cx // 2 * 3, cy // 2 + 2 * T, cz)
        vmem = pltpu.VMEM
        call = pl.pallas_call(
            functools.partial(kernel, sizes),
            out_shape=jax.ShapeDtypeStruct(source.shape, F32),
            in_specs=[pl.BlockSpec(memory_space=vmem)] * 2,
            out_specs=pl.BlockSpec(memory_space=vmem),
            scratch_shapes=[
                vmem((2,) + fine, F32),
                vmem((cy, cz), F32),
                vmem((cy, cz), F32),
                vmem((cy, cz), F32),
                vmem((3, cy + 2 * T, cz), F32),
                vmem(fine, F32),
                vmem(fine, F32),
                vmem(fine, F32),
                vmem(fine, F32),
                vmem(fine, F32),
                vmem(fine, F32),
                vmem((3, cx // 2, cy // 2, cz), F32),
                vmem((3, cx // 2, cy // 2, cz), F32),
                vmem((3, cx // 2, cy // 2, cz), F32),
                vmem((3,) + mid, F32),
                vmem((2, 2, cx // 4, cy // 4, cz), F32),
                vmem((2, cx // 2, cy // 2, cz), F32),
                pltpu.SemaphoreType.DMA((copies,)),
                pltpu.SemaphoreType.DMA((copies,)),
            ],
            compiler_params=pltpu.CompilerParams(
                collective_id=0, has_side_effects=True, vmem_limit_bytes=48 * 2**20
            ),
        )
        return call(source, conductivity)

    return jax.shard_map(
        local, mesh=mesh, in_specs=(spec, spec), out_specs=spec, check_vma=False
    )
```

time: 332 us -> 50.3 us (0.15); the launches traced: 327 us -> 50.1 us
  starting transfers between devices: 233 us -> 0 us
  waiting for transfers between devices: 62.7 us -> 0 us
  Pallas kernels: 0 us -> 47.6 us
  local copies, waits for them, and re-layouts: 18.9 us -> 2.47 us
  other arithmetic: 10.7 us -> 0 us
    ppermute x81 -> x0, starting transfers between devices: 233 us -> none  [the longest x39 162 us: padded_2(): lax.ppermute(tail, axis, [(i, (i + 1) % count) for i in range(ends)])]
    ppermute x81 -> x0, waiting for transfers between devices: 62.7 us -> none  [the longest x39 33.6 us: padded_2(): lax.ppermute(head, axis, [((i + 1) % count, i) for i in range(ends)])]
    pallas_call x0 -> x1, Pallas kernels: none -> 47.6 us  [local(): return call(source, conductivity)]
    reshape x2 -> x0, local copies, waits for them, and re-layouts: 10.7 us -> none  [the longest x1 10.5 us: coarsen(): values.reshape(first // 2, 2, second // 2, 2, third // 2, 2)]
    slice x43 -> x0, local copies, waits for them, and re-layouts: 5.22 us -> none  [the longest x16 3.19 us: restrict_axis(): lax.slice_in_dim(values, start_cell, start_cell + 2 * cells - 1, stride=2...]
    reduce_sum x2 -> x0, other arithmetic: 4.16 us -> none  [coarsen(): values.reshape(first // 2, 2, second // 2, 2, third // 2, 2)]
  transfers between devices with their start and end apart: 81 -> 0, of which waited for: 44 -> 0; matrix products, arithmetic and copies ran while one was open for 6% -> 0% of each run, Pallas kernels for 0% -> 0%
where the time goes in v1:
time: 50.3 us; the launch traced here: 50.1 us
  Pallas kernels  47.6 us (95%)
  local copies, waits for them, and re-layouts  2.47 us (5%)
    pallas_call x1, Pallas kernels, local(): return call(source, conductivity)  47.6 us
    unnamed x5, local copies, waits for them, and re-layouts  2.47 us

profile of v1, /device:TPU:1, one launch (start us, length us, event | category | flops | bytes accessed | tf_op | source)
XLA Modules:
  0.0 50.1 jit_solution(18265689865471668005)
XLA Ops:
  0.0 0.0 copy-start
  0.0 0.9 %copy-done = f32[8,32,128]{2,1,0:T(8,128)S(1)} copy-done((f32[8,32,128]{2,1,0:T(8,128)S(1)}, f32[8,32,128]{2,1,0:T(8,128)}, u32[]{:S(2)}) %copy-start) | copy-done | bytes 131096
  0.9 0.0 copy-start.1
  0.9 0.9 %copy-done.1 = f32[8,32,128]{2,1,0:T(8,128)S(1)} copy-done((f32[8,32,128]{2,1,0:T(8,128)S(1)}, f32[8,32,128]{2,1,0:T(8,128)}, u32[]{:S(2)}) %copy-start.1) | copy-done | bytes 131096
  1.8 47.6 %shard_map.28 = f32[8,32,128]{2,1,0:T(8,128)S(1)} custom-call(f32[8,32,128]{2,1,0:T(8,128)S(1)} %copy-done, f32[8,32,128]{2,1,0:T(8,128)S(1)} %copy-done.1), custom_call_target="tpu_custom_call" | custom-call | tf_op jit(solution)/shard_map/pallas_call | solution.py:463
  49.5 0.7 %copy.4 = f32[8,32,128]{2,1,0:T(8,128)} copy(f32[8,32,128]{2,1,0:T(8,128)S(1)} %shard_map.28) | data formatting | bytes 262144
Async XLA Ops:
  0.0 0.9 %copy-start = (f32[8,32,128]{2,1,0:T(8,128)S(1)}, f32[8,32,128]{2,1,0:T(8,128)}, u32[]{:S(2)}) copy-start(f32[8,32,128]{2,1,0:T(8,128)} %s_ref.1) | copy-start | bytes 393220
  0.9 0.9 %copy-start.1 = (f32[8,32,128]{2,1,0:T(8,128)S(1)}, f32[8,32,128]{2,1,0:T(8,128)}, u32[]{:S(2)}) copy-start(f32[8,32,128]{2,1,0:T(8,128)} %k_ref.1) | copy-start | bytes 393220

commit v2 on v1

v2 whole, which is shorter than its diff:
```python
import functools
import math

import jax
import jax.numpy as jnp
from jax import lax
from jax.experimental import pallas as pl
from jax.experimental.pallas import tpu as pltpu
from jax.sharding import PartitionSpec as P

spectrum_top = 1.9
spectrum_low = 0.475
omega_first = 1.0 / (
    (spectrum_top + spectrum_low) / 2 + (spectrum_top - spectrum_low) / 2 * math.cos(math.pi / 4)
)
omega_second = 1.0 / (
    (spectrum_top + spectrum_low) / 2
    + (spectrum_top - spectrum_low) / 2 * math.cos(3 * math.pi / 4)
)
F32 = jnp.float32
MESH = pl.DeviceIdType.MESH
H = 4
T = 8


def iota(shape, dim):
    return lax.broadcasted_iota(jnp.int32, shape, dim)


def parts(values):
    high = values.astype(jnp.bfloat16)
    rest = values - high.astype(F32)
    middle = rest.astype(jnp.bfloat16)
    return [high, middle, (rest - middle.astype(F32)).astype(jnp.bfloat16)]


def times(values, weights):
    size = values.shape[0]
    result = jnp.dot(
        jnp.concatenate(parts(values), axis=0),
        weights.astype(jnp.bfloat16),
        preferred_element_type=F32,
    )
    return result[:size] + (result[size : 2 * size] + result[2 * size :])


def weigh(weights, values):
    return jnp.dot(
        jnp.concatenate([weights.astype(jnp.bfloat16)] * 3, axis=1),
        jnp.concatenate(parts(values), axis=0),
        preferred_element_type=F32,
    )


def ring(index, size, cut):
    return jnp.where(index >= cut, index - size, index)


def restrict_weight(diff):
    side = (diff == -1) | (diff == 2)
    centre = (diff == 0) | (diff == 1)
    return jnp.where(centre, 0.375, jnp.where(side, 0.125, 0.0)).astype(F32)


def mean_weight(diff):
    return jnp.where((diff == 0) | (diff == 1), 0.5, 0.0).astype(F32)


def interpolate_weight(fine, coarse):
    base = (fine + 64) // 2 - 32
    other = base + jnp.where((fine + 64) % 2 == 0, -1, 1)
    return jnp.where(coarse == base, 0.75, jnp.where(coarse == other, 0.25, 0.0)).astype(F32)


def shift(values, axis, amount):
    size = values.shape[axis]
    return pltpu.roll(values, (-amount) % size, axis)


def span(way, extent, halo):
    if way == 0:
        return pl.ds(halo, extent), pl.ds(halo, extent)
    if way > 0:
        return pl.ds(extent, halo), pl.ds(0, halo)
    return pl.ds(halo, halo), pl.ds(halo + extent, halo)


ways = (0, 1, -1)
others = [(a, b, c) for c in ways for b in ways for a in ways if (a, b, c) != (0, 0, 0)]
mates = [(a, b, c) for a in (0, 1) for b in (0, 1) for c in (0, 1) if (a, b, c) != (0, 0, 0)]
axes = ("gx", "gy", "gz")
copies = 4 * len(others) + 2 * len(mates)


def kernel(
    sizes, s_ref, k_ref, out_ref,
    ks, pk, qa, qb, wx, wy, wz, iv, ua, ub, rs, fs, cs,
    mid, mp, ma, mb, cg, send_sem, recv_sem,
):
    cx, cy, cz_ = s_ref.shape
    hx, hy, hz = cx // 2, cy // 2, cz_ // 2
    qx, qy, qz = cx // 4, cy // 4, cz_ // 4
    ex, ey, ez = ks.shape[1:]
    mx, my, mz = mid.shape[1:]
    pos = {axis: lax.axis_index(axis) for axis in axes}
    used = [0]

    def has(offset, sign):
        here = None
        for axis, way in zip(axes, offset):
            if way != 0:
                good = pos[axis] < sizes[axis] - 1 if way * sign > 0 else pos[axis] > 0
                here = good if here is None else here & good
        return here

    def make(offset, src, dst, number):
        return pltpu.make_async_remote_copy(
            src_ref=src, dst_ref=dst, send_sem=send_sem.at[number], recv_sem=recv_sem.at[number],
            device_id={axis: pos[axis] + way for axis, way in zip(axes, offset)},
            device_id_type=MESH,
        )

    def start(items):
        started = []
        for offset, src, dst in items:
            number = used[0]
            used[0] += 1
            started.append((offset, src, dst, number))

            @pl.when(has(offset, 1))
            def _():
                make(offset, src, dst, number).start()

        return started

    def finish_recv(started):
        for offset, src, dst, number in started:

            @pl.when(has(offset, -1))
            def _():
                make(offset, src, dst, number).wait_recv()

    def finish_send(started):
        for offset, src, dst, number in started:

            @pl.when(has(offset, 1))
            def _():
                make(offset, src, dst, number).wait_send()

    def clear(i, carry):
        ks[0, i] = jnp.zeros((ey, ez), F32)
        ks[1, i] = jnp.zeros((ey, ez), F32)
        return carry

    lax.fori_loop(0, ex, clear, 0)
    qa[...] = jnp.zeros(qa.shape, F32)
    qb[...] = jnp.zeros(qb.shape, F32)
    mid[...] = jnp.zeros(mid.shape, F32)
    ma[...] = jnp.zeros(ma.shape, F32)
    mb[...] = jnp.zeros(mb.shape, F32)
    barrier = pltpu.get_barrier_semaphore()
    count = 0
    for offset in others:
        here = has(offset, 1)
        count = count + here.astype(jnp.int32)

        @pl.when(here)
        def _():
            pl.semaphore_signal(
                barrier, inc=1,
                device_id={axis: pos[axis] + way for axis, way in zip(axes, offset)},
                device_id_type=MESH,
            )

    group = iota((cy, cz_), 1) // (2 * H)
    packed = jnp.zeros((cy, cz_), F32)
    for f, ref in enumerate((k_ref, s_ref)):
        for p in range(cx):
            g = f * cx + p
            ks[f, H + p, T : T + cy, 0:cz_] = ref[p]
            packed = jnp.where(group == g, shift(ref[p], 1, -(H + 2 * H * g)), packed)
    pk[...] = packed
    pl.semaphore_wait(barrier, count)

    main = pl.ds(0, cz_)
    items = []
    for offset in others:
        dx, dy, dz = offset
        xs, xd = span(dx, cx, H)
        ys, yd = span(dy, cy, T)
        if dz == 0:
            items.append((offset, ks.at[:, xs, ys, main], ks.at[:, xd, yd, main]))
        else:
            target = qa if dz > 0 else qb
            rows = pl.ds(ys.start - T, ys.size)
            items.append((offset, pk.at[rows], target.at[1 - dx, yd]))
    fine_round = start(items)

    mgroup = iota((hy, mz), 1) // H

    def middle_start(f):
        packed = jnp.zeros((hy, mz), F32)
        for p in range(hx):
            own = mid[f, hx + p, T : T + hy, :]
            packed = jnp.where(mgroup == 2 * p, shift(own, 1, hz - H - 2 * H * p), packed)
            packed = jnp.where(mgroup == 2 * p + 1, shift(own, 1, -(2 * H * p + H)), packed)
        mp[f] = packed
        items = []
        for offset in others:
            dx, dy, dz = offset
            xs, xd = span(dx, hx, hx)
            ys, yd = span(dy, hy, T)
            if dz == 0:
                items.append((offset, mid.at[f, xs, ys], mid.at[f, xd, yd]))
            else:
                target = ma if dz > 0 else mb
                rows = pl.ds(ys.start - T, ys.size)
                items.append((offset, mp.at[f, rows], target.at[f, 1 - dx, yd]))
        return start(items)

    mlane = iota((my, mz), 1)

    def middle_finish(f, started):
        finish_recv(started)
        planes = []
        for i in range(mx):
            block, p = i // hx, i % hx
            right = shift(mb[f, block], 1, 2 * H * p + H - hz)
            left = shift(ma[f, block], 1, 2 * H * p - (mz - H))
            side = jnp.where(mlane < (hz + mz) // 2, right, left)
            planes.append(jnp.where(mlane < hz, mid[f, i], side)[None])
        return jnp.concatenate(planes, axis=0)

    px, py, pz = (pos[axis] % 2 for axis in axes)
    here = pl.ds(px * qx, qx)
    line = pl.ds(pl.multiple_of(py * qy, qy), qy)

    def gather_make(f, flips, number):
        return pltpu.make_async_remote_copy(
            src_ref=cg.at[f, 0, here, line], dst_ref=cg.at[f, flips[2], here, line],
            send_sem=send_sem.at[number], recv_sem=recv_sem.at[number],
            device_id={
                axis: pos[axis] + (1 - 2 * (pos[axis] % 2)) * flip for axis, flip in zip(axes, flips)
            },
            device_id_type=MESH,
        )

    def gather_start(f):
        started = []
        for flips in mates:
            copy = gather_make(f, flips, used[0])
            used[0] += 1
            copy.start()
            started.append(copy)
        return started

    lz = iota((cz_, mz), 0) - 2 * iota((cz_, mz), 1)
    mean_z = jnp.where(iota((cz_, mz), 1) < hz, mean_weight(lz), 0.0)
    for i in range(hx):
        rs[0, i, T : T + cy, :] = (k_ref[2 * i] + k_ref[2 * i + 1]) * 0.5
    means = [
        (rs[0, i, pl.ds(T, hy, stride=2), :] + rs[0, i, pl.ds(T + 1, hy, stride=2), :]) * 0.5
        for i in range(hx)
    ]
    means = times(jnp.concatenate(means, axis=0), mean_z)
    for i in range(hx):
        mid[0, hx + i, T : T + hy, :] = means[i * hy : (i + 1) * hy]
    coeff_round = middle_start(0)

    cj = iota((mz, mz), 1) - pz * qz
    clz = ring(iota((mz, mz), 0), mz, (hz + mz) // 2) - 2 * cj
    ckeep = (cj >= 0) & (cj < qz)
    to_coarse_z = jnp.where(ckeep, restrict_weight(clz), 0.0)
    cmean_z = jnp.where(ckeep, mean_weight(clz), 0.0)
    for i in range(qx):
        own_rows = [mid[0, hx + 2 * i + j, T : T + hy, :] for j in range(2)]
        cs[i, T : T + hy, :] = (own_rows[0] + own_rows[1]) * 0.5
    means = [
        (cs[i, pl.ds(T, qy, stride=2), :] + cs[i, pl.ds(T + 1, qy, stride=2), :]) * 0.5
        for i in range(qx)
    ]
    means = times(jnp.concatenate(means, axis=0), cmean_z)
    for i in range(qx):
        cg[0, 0, px * qx + i, line, :] = means[i * qy : (i + 1) * qy]
    gather_coeff = gather_start(0)

    r = iota((ey, ez), 0) - T + pos["gy"] * cy
    local_z = ring(iota((ey, ez), 1), ez, ez - cz_ // 2)
    z = local_z + pos["gz"] * cz_
    fine_in = (r >= 0) & (r < cy * sizes["gy"]) & (z >= 0) & (z < cz_ * sizes["gz"])
    fine_in = fine_in & (local_z >= -H) & (local_z < cz_ + H)

    def plane_in(i):
        x = i - H + pos["gx"] * cx
        return (x >= 0) & (x < cx * sizes["gx"])

    finish_recv(fine_round)
    lane = iota((ey, cz_), 1)
    for block in range(3):
        merged = jnp.where(lane % (2 * H) < H, qa[block], qb[block])
        for i in range(ex):
            if (i - H) // cx + 1 == block:
                for f in range(2):
                    p = (i - H) % cx
                    ks[f, i, :, cz_:ez] = shift(merged, 1, H + 2 * H * (f * cx + p))

    wx[0] = 0.5 * (ks[0, 0] + ks[0, 1])

    def weights(i, carry):
        k = ks[0, i]
        after = 0.5 * (k + ks[0, i + 1])
        a = 0.5 * (k + shift(k, 0, 1))
        b = 0.5 * (k + shift(k, 1, 1))
        diag = (wx[i - 1] + after) + (a + shift(a, 0, -1)) + (b + shift(b, 1, -1))
        wx[i] = after
        wy[i] = a
        wz[i] = b
        inverse = jnp.where(fine_in & plane_in(i), 1.0 / diag, 0.0)
        iv[i] = inverse
        ua[i] = omega_first * ks[1, i] * inverse
        return carry

    lax.fori_loop(1, ex - 1, weights, 0, unroll=2)

    def around(u, i):
        v = u[i]
        a, b = wy[i], wz[i]
        total = wx[i] * u[i + 1] + wx[i - 1] * u[i - 1]
        total = total + (a * shift(v, 0, 1) + shift(a * v, 0, -1))
        total = total + (b * shift(v, 1, 1) + shift(b * v, 1, -1))
        return v, total

    def fine_sweep(u, i, omega):
        v, total = around(u, i)
        return (1.0 - omega) * v + omega * (ks[1, i] + total) * iv[i]

    def pre(i, carry):
        ub[i] = fine_sweep(ua, i, omega_second)
        return carry

    lax.fori_loop(2, ex - 2, pre, 0, unroll=2)

    def leftover(i, carry):
        v, total = around(ub, i)
        inverse = iv[i]
        diag = wx[i] + wx[i - 1] + (wy[i] + shift(wy[i], 0, -1)) + (wz[i] + shift(wz[i], 1, -1))
        ua[i] = jnp.where(inverse > 0.0, ks[1, i] - diag * v + total, 0.0)
        return carry

    lax.fori_loop(3, ex - 3, leftover, 0, unroll=2)

    lz = ring(iota((ez, mz), 0), ez, ez - cz_ // 2) - 2 * iota((ez, mz), 1)
    to_middle_z = jnp.where(iota((ez, mz), 1) < hz, restrict_weight(lz), 0.0)

    def restrict_rows(take):
        side = take(T - 1) + take(T + 2)
        return side * 0.125 + (take(T) + take(T + 1)) * 0.375

    pieces = []
    for i in range(hx):
        c = H + 2 * i
        mixed = (ua[c - 1] + ua[c + 2]) * 0.5 + (ua[c] + ua[c + 1]) * 1.5
        rs[0, i] = mixed[:, :cz_]
        rs[1, i] = mixed[:, cz_:]
        halves = [
            restrict_rows(lambda first: rs[t, i, pl.ds(first, hy, stride=2), :]) for t in range(2)
        ]
        pieces.append(jnp.concatenate(halves, axis=1))
    rhs = times(jnp.concatenate(pieces, axis=0), to_middle_z)
    for i in range(hx):
        mid[1, hx + i, T : T + hy, :] = rhs[i * hy : (i + 1) * hy]
    rhs_round = middle_start(1)

    mr = iota((mx, my, mz), 1) - T + pos["gy"] * hy
    mlz = ring(iota((mx, my, mz), 2), mz, (hz + mz) // 2)
    mzz = mlz + pos["gz"] * hz
    mxx = iota((mx, my, mz), 0) - hx + pos["gx"] * hx
    middle_in = (
        (mr >= 0) & (mr < hy * sizes["gy"]) & (mzz >= 0) & (mzz < hz * sizes["gz"])
        & (mxx >= 0) & (mxx < hx * sizes["gx"]) & (mlz >= -H) & (mlz < hz + H)
    )

    def up(values):
        return jnp.concatenate([values[1:], values[:1]], axis=0)

    def down(values):
        return jnp.concatenate([values[-1:], values[:-1]], axis=0)

    def faces(k):
        return 0.5 * (k + up(k)), 0.5 * (k + shift(k, 1, 1)), 0.5 * (k + shift(k, 2, 1))

    def diagonal(w):
        return (w[0] + down(w[0])) + (w[1] + shift(w[1], 1, -1)) + (w[2] + shift(w[2], 2, -1))

    def neighbours(w, v):
        total = w[0] * up(v) + down(w[0] * v)
        total = total + (w[1] * shift(v, 1, 1) + shift(w[1] * v, 1, -1))
        return total + (w[2] * shift(v, 2, 1) + shift(w[2] * v, 2, -1))

    def sweep(w, inverse, v, f, omega):
        return (1.0 - omega) * v + omega * (f + neighbours(w, v)) * inverse

    mk = middle_finish(0, coeff_round)
    mw = faces(mk)
    mdiag = diagonal(mw)
    miv = jnp.where(middle_in, 1.0 / mdiag, 0.0)

    for copy in gather_coeff:
        copy.wait_recv()
    ck = cg[0, 0] + cg[0, 1]
    cshape = ck.shape
    row = iota(cshape, 1)
    plane = iota(cshape, 0)
    box_in = iota(cshape, 2) < 2 * qz
    nx, ny = 2 * qx, 2 * qy
    cw = faces(ck)
    half = 0.5 * ck
    cwx = jnp.where(plane < nx - 1, cw[0], 0.0)
    cwy = jnp.where(row < ny - 1, cw[1], 0.0)
    cw = (cwx, cwy, cw[2])
    cdiag = diagonal(cw)
    cdiag = cdiag + jnp.where(plane == 0, half, 0.0) + jnp.where(plane == nx - 1, half, 0.0)
    cdiag = cdiag + jnp.where(row == 0, half, 0.0) + jnp.where(row == ny - 1, half, 0.0)
    civ = jnp.where(box_in, 1.0 / cdiag, 0.0)

    mf = middle_finish(1, rhs_round)
    m1 = omega_first * mf * miv
    m2 = sweep(mw, miv, m1, mf, omega_second)
    mleft = jnp.where(middle_in, mf - mdiag * m2 + neighbours(mw, m2), 0.0)

    pieces = []
    for i in range(qx):
        c = hx + 2 * i
        cs[i] = (mleft[c - 1] + mleft[c + 2]) * 0.5 + (mleft[c] + mleft[c + 1]) * 1.5
        pieces.append(restrict_rows(lambda first: cs[i, pl.ds(first, qy, stride=2), :]))
    rhs = times(jnp.concatenate(pieces, axis=0), to_coarse_z)
    for i in range(qx):
        cg[1, 0, px * qx + i, line, :] = rhs[i * qy : (i + 1) * qy]
    gather_rhs = gather_start(1)
    for copy in gather_rhs:
        copy.wait_recv()

    cf = cg[1, 0] + cg[1, 1]
    c1 = omega_first * cf * civ
    c2 = sweep(cw, civ, c1, cf, omega_second)
    flat = c2.reshape(nx * ny, mz)
    jj = iota((mz, mz), 1)
    back_z = interpolate_weight(jj + pz * hz, iota((mz, mz), 0))
    back_z = jnp.where((jj < hz) & (iota((mz, mz), 0) < 2 * qz), back_z, 0.0)
    shape = (hx * hy, nx * ny)
    fine_i, coarse_i = iota(shape, 0), iota(shape, 1)
    back_xy = interpolate_weight(fine_i // hy + px * hx, coarse_i // ny) * interpolate_weight(
        fine_i % hy + py * hy, coarse_i % ny
    )
    correction = weigh(back_xy, times(flat, back_z))
    for i in range(hx):
        fixed = m2[hx + i, T : T + hy, :] + correction[i * hy : (i + 1) * hy]
        mid[2, hx + i, T : T + hy, :] = fixed
    last_round = middle_start(2)
    m3 = middle_finish(2, last_round)
    m4 = sweep(mw, miv, m3, mf, omega_first)
    m5 = sweep(mw, miv, m4, mf, omega_second)

    fine_lane = ring(iota((mz, ez), 1), ez, ez - cz_ // 2)
    middle_lane = ring(iota((mz, ez), 0), mz, (hz + mz) // 2)
    wide = (fine_lane >= -H) & (fine_lane < cz_ + H)
    to_fine_z = jnp.where(wide, interpolate_weight(fine_lane, middle_lane), 0.0)
    low = hx - 2
    spread = times(m5[low : 2 * hx + 2].reshape((hx + 4) * my, mz), to_fine_z)
    for i in range(2, ex - 2):
        c = (i - H + 64) // 2 - 32 + hx - low
        other = c - 1 if i % 2 == 0 else c + 1
        mixed = 0.75 * spread[c * my : (c + 1) * my] + 0.25 * spread[other * my : (other + 1) * my]
        near = 0.75 * mixed
        even = near + 0.25 * shift(mixed, 0, -1)
        odd = near + 0.25 * shift(mixed, 0, 1)
        for t in range(2):
            lanes = slice(t * cz_, (t + 1) * cz_)
            fs[t, i - 2, pl.ds(0, my, stride=2), :] = even[:, lanes]
            fs[t, i - 2, pl.ds(1, my, stride=2), :] = odd[:, lanes]
    for i in range(2, ex - 2):
        rows = slice(2 * T - T, 2 * T - T + ey)
        fresh = jnp.concatenate([fs[0, i - 2, rows, :], fs[1, i - 2, rows, :]], axis=1)
        ua[i] = jnp.where(fine_in & plane_in(i), ub[i] + fresh, 0.0)

    def post(i, carry):
        ub[i] = fine_sweep(ua, i, omega_first)
        return carry

    lax.fori_loop(3, ex - 3, post, 0, unroll=2)

    def last(i, carry):
        out_ref[i - H] = fine_sweep(ub, i, omega_second)[T : T + cy, 0:cz_]
        return carry

    lax.fori_loop(H, H + cx, last, 0, unroll=2)
    for started in (fine_round, coeff_round, rhs_round, last_round):
        finish_send(started)
    for copy in gather_coeff + gather_rhs:
        copy.wait_send()


def solution(mesh):
    sizes = {axis: mesh.shape[axis] for axis in mesh.axis_names}
    spec = P("gx", "gy", "gz")

    def local(source, conductivity):
        cx, cy, cz = source.shape
        fine = (cx + 2 * H, cy + 2 * T, 2 * cz)
        mid = (cx // 2 * 3, cy // 2 + 2 * T, cz)
        vmem = pltpu.VMEM
        call = pl.pallas_call(
            functools.partial(kernel, sizes),
            out_shape=jax.ShapeDtypeStruct(source.shape, F32),
            in_specs=[pl.BlockSpec(memory_space=vmem)] * 2,
            out_specs=pl.BlockSpec(memory_space=vmem),
            scratch_shapes=[
                vmem((2,) + fine, F32),
                vmem((cy, cz), F32),
                vmem((3, cy + 2 * T, cz), F32),
                vmem((3, cy + 2 * T, cz), F32),
                vmem(fine, F32),
                vmem(fine, F32),
                vmem(fine, F32),
                vmem(fine, F32),
                vmem(fine, F32),
                vmem(fine, F32),
                vmem((2, cx // 2, cy + 2 * T, cz), F32),
                vmem((2, cx + 4, 2 * mid[1], cz), F32),
                vmem((cx // 4, mid[1], cz), F32),
                vmem((3,) + mid, F32),
                vmem((3, cy // 2, cz), F32),
                vmem((3, 3) + mid[1:], F32),
                vmem((3, 3) + mid[1:], F32),
                vmem((2, 2, cx // 2, cy // 2, cz), F32),
                pltpu.SemaphoreType.DMA((copies,)),
                pltpu.SemaphoreType.DMA((copies,)),
            ],
            compiler_params=pltpu.CompilerParams(
                collective_id=0, has_side_effects=True, vmem_limit_bytes=48 * 2**20
            ),
        )
        return call(source, conductivity)

    return jax.shard_map(
        local, mesh=mesh, in_specs=(spec, spec), out_specs=spec, check_vma=False
    )
```

time: 50.3 us -> 33.4 us (0.66)
  Pallas kernels: 47.6 us -> 30.8 us
    pallas_call x1, Pallas kernels: 47.6 us -> 30.8 us  [local(): return call(source, conductivity)]
where the time goes in v2:
time: 33.4 us; the launch traced here: 33.2 us
  Pallas kernels  30.8 us (92%)
  local copies, waits for them, and re-layouts  2.47 us (7%)
    pallas_call x1, Pallas kernels, local(): return call(source, conductivity)  30.8 us
    unnamed x5, local copies, waits for them, and re-layouts  2.47 us

profile of v2, /device:TPU:1, one launch (start us, length us, event | category | flops | bytes accessed | tf_op | source)
XLA Modules:
  0.0 33.2 jit_solution(2973566607909035419)
XLA Ops:
  0.0 0.0 copy-start
  0.0 0.9 %copy-done = f32[8,32,128]{2,1,0:T(8,128)S(1)} copy-done((f32[8,32,128]{2,1,0:T(8,128)S(1)}, f32[8,32,128]{2,1,0:T(8,128)}, u32[]{:S(2)}) %copy-start) | copy-done | bytes 131096
  0.9 0.0 copy-start.1
  0.9 0.9 %copy-done.1 = f32[8,32,128]{2,1,0:T(8,128)S(1)} copy-done((f32[8,32,128]{2,1,0:T(8,128)S(1)}, f32[8,32,128]{2,1,0:T(8,128)}, u32[]{:S(2)}) %copy-start.1) | copy-done | bytes 131096
  1.8 30.8 %shard_map.28 = f32[8,32,128]{2,1,0:T(8,128)S(1)} custom-call(f32[8,32,128]{2,1,0:T(8,128)S(1)} %copy-done, f32[8,32,128]{2,1,0:T(8,128)S(1)} %copy-done.1), custom_call_target="tpu_custom_call" | custom-call | tf_op jit(solution)/shard_map/pallas_call | solution.py:543
  32.6 0.7 %copy.4 = f32[8,32,128]{2,1,0:T(8,128)} copy(f32[8,32,128]{2,1,0:T(8,128)S(1)} %shard_map.28) | data formatting | bytes 262144
Async XLA Ops:
  0.0 0.9 %copy-start = (f32[8,32,128]{2,1,0:T(8,128)S(1)}, f32[8,32,128]{2,1,0:T(8,128)}, u32[]{:S(2)}) copy-start(f32[8,32,128]{2,1,0:T(8,128)} %s_ref.1) | copy-start | bytes 393220
  0.9 0.9 %copy-start.1 = (f32[8,32,128]{2,1,0:T(8,128)S(1)}, f32[8,32,128]{2,1,0:T(8,128)}, u32[]{:S(2)}) copy-start(f32[8,32,128]{2,1,0:T(8,128)} %k_ref.1) | copy-start | bytes 393220

commit v3 on v2

--- a/solution.py
+++ b/solution.py
@@ -94,8 +94,8 @@
 
 def kernel(
     sizes, s_ref, k_ref, out_ref,
-    ks, pk, qa, qb, wx, wy, wz, iv, ua, ub, rs, fs, cs,
-    mid, mp, ma, mb, cg, send_sem, recv_sem,
+    ks, pk, qa, qb, wx, wy, wz, iv, ua, ub, left, rs, fs, cs,
+    mid, mp, ma, mb, cg, send_sem, recv_sem, load_sem,
 ):
     cx, cy, cz_ = s_ref.shape
     hx, hy, hz = cx // 2, cy // 2, cz_ // 2
@@ -133,8 +133,10 @@
 
         return started
 
-    def finish_recv(started):
+    def finish_recv(started, wanted=lambda offset: True):
         for offset, src, dst, number in started:
+            if not wanted(offset):
+                continue
 
             @pl.when(has(offset, -1))
             def _():
@@ -147,12 +149,18 @@
             def _():
                 make(offset, src, dst, number).wait_send()
 
-    def clear(i, carry):
-        ks[0, i] = jnp.zeros((ey, ez), F32)
-        ks[1, i] = jnp.zeros((ey, ez), F32)
-        return carry
-
-    lax.fori_loop(0, ex, clear, 0)
+    loads = []
+    for f, ref in enumerate((k_ref, s_ref)):
+        own = ks.at[f, pl.ds(H, cx), pl.ds(T, cy), pl.ds(0, cz_)]
+        loads.append(pltpu.make_async_copy(ref, own, load_sem.at[f]))
+        loads[f].start()
+    for f in range(2):
+        for i in range(ex):
+            if H <= i < H + cx:
+                ks[f, i, 0:T, 0:cz_] = jnp.zeros((T, cz_), F32)
+                ks[f, i, T + cy : ey, 0:cz_] = jnp.zeros((T, cz_), F32)
+            else:
+                ks[f, i, :, 0:cz_] = jnp.zeros((ey, cz_), F32)
     qa[...] = jnp.zeros(qa.shape, F32)
     qb[...] = jnp.zeros(qb.shape, F32)
     mid[...] = jnp.zeros(mid.shape, F32)
@@ -174,11 +182,12 @@
 
     group = iota((cy, cz_), 1) // (2 * H)
     packed = jnp.zeros((cy, cz_), F32)
-    for f, ref in enumerate((k_ref, s_ref)):
+    for f in range(2):
+        loads[f].wait()
         for p in range(cx):
             g = f * cx + p
-            ks[f, H + p, T : T + cy, 0:cz_] = ref[p]
-            packed = jnp.where(group == g, shift(ref[p], 1, -(H + 2 * H * g)), packed)
+            own = ks[f, H + p, T : T + cy, 0:cz_]
+            packed = jnp.where(group == g, shift(own, 1, -(H + 2 * H * g)), packed)
     pk[...] = packed
     pl.semaphore_wait(barrier, count)
 
@@ -257,7 +266,8 @@
     lz = iota((cz_, mz), 0) - 2 * iota((cz_, mz), 1)
     mean_z = jnp.where(iota((cz_, mz), 1) < hz, mean_weight(lz), 0.0)
     for i in range(hx):
-        rs[0, i, T : T + cy, :] = (k_ref[2 * i] + k_ref[2 * i + 1]) * 0.5
+        own = [ks[0, H + 2 * i + j, T : T + cy, 0:cz_] for j in range(2)]
+        rs[0, i, T : T + cy, :] = (own[0] + own[1]) * 0.5
     means = [
         (rs[0, i, pl.ds(T, hy, stride=2), :] + rs[0, i, pl.ds(T + 1, hy, stride=2), :]) * 0.5
         for i in range(hx)
@@ -294,17 +304,40 @@
         x = i - H + pos["gx"] * cx
         return (x >= 0) & (x < cx * sizes["gx"])
 
-    finish_recv(fine_round)
+    lz = ring(iota((ez, mz), 0), ez, ez - cz_ // 2) - 2 * iota((ez, mz), 1)
+    to_middle_z = jnp.where(iota((ez, mz), 1) < hz, restrict_weight(lz), 0.0)
+
+    mr = iota((mx, my, mz), 1) - T + pos["gy"] * hy
+    mlz = ring(iota((mx, my, mz), 2), mz, (hz + mz) // 2)
+    mzz = mlz + pos["gz"] * hz
+    mxx = iota((mx, my, mz), 0) - hx + pos["gx"] * hx
+    middle_in = (
+        (mr >= 0) & (mr < hy * sizes["gy"]) & (mzz >= 0) & (mzz < hz * sizes["gz"])
+        & (mxx >= 0) & (mxx < hx * sizes["gx"]) & (mlz >= -H) & (mlz < hz + H)
+    )
+
+    jj = iota((mz, mz), 1)
+    back_z = interpolate_weight(jj + pz * hz, iota((mz, mz), 0))
+    back_z = jnp.where((jj < hz) & (iota((mz, mz), 0) < 2 * qz), back_z, 0.0)
+    shape = (hx * hy, 4 * qx * qy)
+    fine_i, coarse_i = iota(shape, 0), iota(shape, 1)
+    back_xy = interpolate_weight(fine_i // hy + px * hx, coarse_i // (2 * qy)) * interpolate_weight(
+        fine_i % hy + py * hy, coarse_i % (2 * qy)
+    )
+    fine_lane = ring(iota((mz, ez), 1), ez, ez - cz_ // 2)
+    middle_lane = ring(iota((mz, ez), 0), mz, (hz + mz) // 2)
+    wide = (fine_lane >= -H) & (fine_lane < cz_ + H)
+    to_fine_z = jnp.where(wide, interpolate_weight(fine_lane, middle_lane), 0.0)
+
     lane = iota((ey, cz_), 1)
-    for block in range(3):
+
+    def unpack(block):
         merged = jnp.where(lane % (2 * H) < H, qa[block], qb[block])
         for i in range(ex):
             if (i - H) // cx + 1 == block:
                 for f in range(2):
                     p = (i - H) % cx
                     ks[f, i, :, cz_:ez] = shift(merged, 1, H + 2 * H * (f * cx + p))
-
-    wx[0] = 0.5 * (ks[0, 0] + ks[0, 1])
 
     def weights(i, carry):
         k = ks[0, i]
@@ -320,8 +353,6 @@
         ua[i] = omega_first * ks[1, i] * inverse
         return carry
 
-    lax.fori_loop(1, ex - 1, weights, 0, unroll=2)
-
     def around(u, i):
         v = u[i]
         a, b = wy[i], wz[i]
@@ -338,19 +369,34 @@
         ub[i] = fine_sweep(ua, i, omega_second)
         return carry
 
-    lax.fori_loop(2, ex - 2, pre, 0, unroll=2)
 
     def leftover(i, carry):
         v, total = around(ub, i)
         inverse = iv[i]
         diag = wx[i] + wx[i - 1] + (wy[i] + shift(wy[i], 0, -1)) + (wz[i] + shift(wz[i], 1, -1))
-        ua[i] = jnp.where(inverse > 0.0, ks[1, i] - diag * v + total, 0.0)
+        left[i] = jnp.where(inverse > 0.0, ks[1, i] - diag * v + total, 0.0)
         return carry
 
-    lax.fori_loop(3, ex - 3, leftover, 0, unroll=2)
-
-    lz = ring(iota((ez, mz), 0), ez, ez - cz_ // 2) - 2 * iota((ez, mz), 1)
-    to_middle_z = jnp.where(iota((ez, mz), 1) < hz, restrict_weight(lz), 0.0)
+    def run(low, high, body):
+        lax.fori_loop(low, high, body, 0, unroll=2)
+
+    last_own = H + cx - 1
+    finish_recv(fine_round, lambda offset: offset[0] == 0)
+    unpack(1)
+    wx[H] = 0.5 * (ks[0, H] + ks[0, H + 1])
+    run(H + 1, last_own, weights)
+    run(H + 2, last_own - 1, pre)
+    run(H + 3, last_own - 2, leftover)
+    finish_recv(fine_round, lambda offset: offset[0] != 0)
+    unpack(0)
+    unpack(2)
+    wx[0] = 0.5 * (ks[0, 0] + ks[0, 1])
+    run(1, H + 1, weights)
+    run(last_own, ex - 1, weights)
+    run(2, H + 2, pre)
+    run(last_own - 1, ex - 2, pre)
+    run(3, H + 3, leftover)
+    run(last_own - 2, ex - 3, leftover)
 
     def restrict_rows(take):
         side = take(T - 1) + take(T + 2)
@@ -359,7 +405,7 @@
     pieces = []
     for i in range(hx):
         c = H + 2 * i
-        mixed = (ua[c - 1] + ua[c + 2]) * 0.5 + (ua[c] + ua[c + 1]) * 1.5
+        mixed = (left[c - 1] + left[c + 2]) * 0.5 + (left[c] + left[c + 1]) * 1.5
         rs[0, i] = mixed[:, :cz_]
         rs[1, i] = mixed[:, cz_:]
         halves = [
@@ -370,15 +416,6 @@
     for i in range(hx):
         mid[1, hx + i, T : T + hy, :] = rhs[i * hy : (i + 1) * hy]
     rhs_round = middle_start(1)
-
-    mr = iota((mx, my, mz), 1) - T + pos["gy"] * hy
-    mlz = ring(iota((mx, my, mz), 2), mz, (hz + mz) // 2)
-    mzz = mlz + pos["gz"] * hz
-    mxx = iota((mx, my, mz), 0) - hx + pos["gx"] * hx
-    middle_in = (
-        (mr >= 0) & (mr < hy * sizes["gy"]) & (mzz >= 0) & (mzz < hz * sizes["gz"])
-        & (mxx >= 0) & (mxx < hx * sizes["gx"]) & (mlz >= -H) & (mlz < hz + H)
-    )
 
     def up(values):
         return jnp.concatenate([values[1:], values[:1]], axis=0)
@@ -423,6 +460,10 @@
     cdiag = cdiag + jnp.where(row == 0, half, 0.0) + jnp.where(row == ny - 1, half, 0.0)
     civ = jnp.where(box_in, 1.0 / cdiag, 0.0)
 
+    finish_send(fine_round)
+    finish_send(coeff_round)
+    for copy in gather_coeff:
+        copy.wait_send()
     mf = middle_finish(1, rhs_round)
     m1 = omega_first * mf * miv
     m2 = sweep(mw, miv, m1, mf, omega_second)
@@ -437,6 +478,7 @@
     for i in range(qx):
         cg[1, 0, px * qx + i, line, :] = rhs[i * qy : (i + 1) * qy]
     gather_rhs = gather_start(1)
+    finish_send(rhs_round)
     for copy in gather_rhs:
         copy.wait_recv()
 
@@ -444,27 +486,17 @@
     c1 = omega_first * cf * civ
     c2 = sweep(cw, civ, c1, cf, omega_second)
     flat = c2.reshape(nx * ny, mz)
-    jj = iota((mz, mz), 1)
-    back_z = interpolate_weight(jj + pz * hz, iota((mz, mz), 0))
-    back_z = jnp.where((jj < hz) & (iota((mz, mz), 0) < 2 * qz), back_z, 0.0)
-    shape = (hx * hy, nx * ny)
-    fine_i, coarse_i = iota(shape, 0), iota(shape, 1)
-    back_xy = interpolate_weight(fine_i // hy + px * hx, coarse_i // ny) * interpolate_weight(
-        fine_i % hy + py * hy, coarse_i % ny
-    )
     correction = weigh(back_xy, times(flat, back_z))
     for i in range(hx):
         fixed = m2[hx + i, T : T + hy, :] + correction[i * hy : (i + 1) * hy]
         mid[2, hx + i, T : T + hy, :] = fixed
     last_round = middle_start(2)
+    for copy in gather_rhs:
+        copy.wait_send()
     m3 = middle_finish(2, last_round)
     m4 = sweep(mw, miv, m3, mf, omega_first)
     m5 = sweep(mw, miv, m4, mf, omega_second)
 
-    fine_lane = ring(iota((mz, ez), 1), ez, ez - cz_ // 2)
-    middle_lane = ring(iota((mz, ez), 0), mz, (hz + mz) // 2)
-    wide = (fine_lane >= -H) & (fine_lane < cz_ + H)
-    to_fine_z = jnp.where(wide, interpolate_weight(fine_lane, middle_lane), 0.0)
     low = hx - 2
     spread = times(m5[low : 2 * hx + 2].reshape((hx + 4) * my, mz), to_fine_z)
     for i in range(2, ex - 2):
@@ -494,10 +526,7 @@
         return carry
 
     lax.fori_loop(H, H + cx, last, 0, unroll=2)
-    for started in (fine_round, coeff_round, rhs_round, last_round):
-        finish_send(started)
-    for copy in gather_coeff + gather_rhs:
-        copy.wait_send()
+    finish_send(last_round)
 
 
 def solution(mesh):
@@ -512,13 +541,14 @@
         call = pl.pallas_call(
             functools.partial(kernel, sizes),
             out_shape=jax.ShapeDtypeStruct(source.shape, F32),
-            in_specs=[pl.BlockSpec(memory_space=vmem)] * 2,
+            in_specs=[pl.BlockSpec(memory_space=pltpu.HBM)] * 2,
             out_specs=pl.BlockSpec(memory_space=vmem),
             scratch_shapes=[
                 vmem((2,) + fine, F32),
                 vmem((cy, cz), F32),
                 vmem((3, cy + 2 * T, cz), F32),
                 vmem((3, cy + 2 * T, cz), F32),
+                vmem(fine, F32),
                 vmem(fine, F32),
                 vmem(fine, F32),
                 vmem(fine, F32),
@@ -535,6 +565,7 @@
                 vmem((2, 2, cx // 2, cy // 2, cz), F32),
                 pltpu.SemaphoreType.DMA((copies,)),
                 pltpu.SemaphoreType.DMA((copies,)),
+                pltpu.SemaphoreType.DMA((2,)),
             ],
             compiler_params=pltpu.CompilerParams(
                 collective_id=0, has_side_effects=True, vmem_limit_bytes=48 * 2**20

time: 33.4 us -> 32.1 us (0.961)
  Pallas kernels: 30.8 us -> 29.5 us
    pallas_call x1, Pallas kernels: 30.8 us -> 29.5 us  [local(): return call(source, conductivity)]
where the time goes in v3:
time: 32.1 us; the launch traced here: 31.9 us
  Pallas kernels  29.5 us (92%)
  local copies, waits for them, and re-layouts  2.47 us (8%)
    pallas_call x1, Pallas kernels, local(): return call(source, conductivity)  29.5 us
    unnamed x5, local copies, waits for them, and re-layouts  2.47 us

profile of v3, /device:TPU:1, one launch (start us, length us, event | category | flops | bytes accessed | tf_op | source)
XLA Modules:
  0.0 31.9 jit_solution(3294065649204992312)
XLA Ops:
  0.0 0.0 copy-start
  0.0 0.9 %copy-done = f32[8,32,128]{2,1,0:T(8,128)S(1)} copy-done((f32[8,32,128]{2,1,0:T(8,128)S(1)}, f32[8,32,128]{2,1,0:T(8,128)}, u32[]{:S(2)}) %copy-start) | copy-done | bytes 131096
  0.9 0.0 copy-start.1
  0.9 0.9 %copy-done.1 = f32[8,32,128]{2,1,0:T(8,128)S(1)} copy-done((f32[8,32,128]{2,1,0:T(8,128)S(1)}, f32[8,32,128]{2,1,0:T(8,128)}, u32[]{:S(2)}) %copy-start.1) | copy-done | bytes 131096
  1.8 29.5 %shard_map.28 = f32[8,32,128]{2,1,0:T(8,128)S(1)} custom-call(f32[8,32,128]{2,1,0:T(8,128)S(1)} %copy-done, f32[8,32,128]{2,1,0:T(8,128)S(1)} %copy-done.1), custom_call_target="tpu_custom_call" | custom-call | tf_op jit(solution)/shard_map/pallas_call | solution.py:574
  31.3 0.7 %copy.4 = f32[8,32,128]{2,1,0:T(8,128)} copy(f32[8,32,128]{2,1,0:T(8,128)S(1)} %shard_map.28) | data formatting | bytes 262144
Async XLA Ops:
  0.0 0.9 %copy-start = (f32[8,32,128]{2,1,0:T(8,128)S(1)}, f32[8,32,128]{2,1,0:T(8,128)}, u32[]{:S(2)}) copy-start(f32[8,32,128]{2,1,0:T(8,128)} %s_ref.1) | copy-start | bytes 393220
  0.9 0.9 %copy-start.1 = (f32[8,32,128]{2,1,0:T(8,128)S(1)}, f32[8,32,128]{2,1,0:T(8,128)}, u32[]{:S(2)}) copy-start(f32[8,32,128]{2,1,0:T(8,128)} %k_ref.1) | copy-start | bytes 393220

commit v4 on v3

--- a/solution.py
+++ b/solution.py
@@ -571,7 +571,7 @@
                 collective_id=0, has_side_effects=True, vmem_limit_bytes=48 * 2**20
             ),
         )
-        return call(source, conductivity)
+        return call(*(pltpu.with_memory_space_constraint(v, pltpu.HBM) for v in (source, conductivity)))
 
     return jax.shard_map(
         local, mesh=mesh, in_specs=(spec, spec), out_specs=spec, check_vma=False

time: 32.1 us -> 30.3 us (0.944)
  local copies, waits for them, and re-layouts: 2.47 us -> 0.66 us
    unnamed x5 -> x1, local copies, waits for them, and re-layouts: 2.47 us -> 0.66 us
where the time goes in v4:
time: 30.3 us; the launch traced here: 30.1 us
  Pallas kernels  29.5 us (97%)
  local copies, waits for them, and re-layouts  0.66 us (2%)
    pallas_call x1, Pallas kernels, local(): call(*(pltpu.with_memory_space_constraint(v, pltpu.HBM) for v in (source,...  29.5 us
    unnamed x1, local copies, waits for them, and re-layouts  0.66 us

profile of v4, /device:TPU:1, one launch (start us, length us, event | category | flops | bytes accessed | tf_op | source)
XLA Modules:
  0.0 30.1 jit_solution(1998587873076767931)
XLA Ops:
  0.0 29.5 %shard_map.28 = f32[8,32,128]{2,1,0:T(8,128)S(1)} custom-call(f32[8,32,128]{2,1,0:T(8,128)} %s_ref.1, f32[8,32,128]{2,1,0:T(8,128)} %k_ref.1), custom_call_target="tpu_custom_call" | custom-call | tf_op jit(solution)/shard_map/pallas_call | solution.py:574
  29.5 0.7 %copy.4 = f32[8,32,128]{2,1,0:T(8,128)} copy(f32[8,32,128]{2,1,0:T(8,128)S(1)} %shard_map.28) | data formatting | bytes 262144

commit v5 on v4

--- a/solution.py
+++ b/solution.py
@@ -94,7 +94,8 @@
 
 def kernel(
     sizes, s_ref, k_ref, out_ref,
-    ks, pk, qa, qb, wx, wy, wz, iv, ua, ub, left, rs, fs, cs,
+    ks, pk, qa, qb, wx, wy, wz, dg, iv, ua, ub, left, rs, fs, cs,
+    mk, mf, mwx, mwy, mwz, mdg, miv, va, vb, vc,
     mid, mp, ma, mb, cg, send_sem, recv_sem, load_sem,
 ):
     cx, cy, cz_ = s_ref.shape
@@ -229,16 +230,14 @@
 
     mlane = iota((my, mz), 1)
 
-    def middle_finish(f, started):
+    def middle_finish(f, started, put):
         finish_recv(started)
-        planes = []
         for i in range(mx):
             block, p = i // hx, i % hx
             right = shift(mb[f, block], 1, 2 * H * p + H - hz)
-            left = shift(ma[f, block], 1, 2 * H * p - (mz - H))
-            side = jnp.where(mlane < (hz + mz) // 2, right, left)
-            planes.append(jnp.where(mlane < hz, mid[f, i], side)[None])
-        return jnp.concatenate(planes, axis=0)
+            left_side = shift(ma[f, block], 1, 2 * H * p - (mz - H))
+            side = jnp.where(mlane < (hz + mz) // 2, right, left_side)
+            put(i, jnp.where(mlane < hz, mid[f, i], side))
 
     px, py, pz = (pos[axis] % 2 for axis in axes)
     here = pl.ds(px * qx, qx)
@@ -307,14 +306,17 @@
     lz = ring(iota((ez, mz), 0), ez, ez - cz_ // 2) - 2 * iota((ez, mz), 1)
     to_middle_z = jnp.where(iota((ez, mz), 1) < hz, restrict_weight(lz), 0.0)
 
-    mr = iota((mx, my, mz), 1) - T + pos["gy"] * hy
-    mlz = ring(iota((mx, my, mz), 2), mz, (hz + mz) // 2)
+    mr = iota((my, mz), 0) - T + pos["gy"] * hy
+    mlz = ring(iota((my, mz), 1), mz, (hz + mz) // 2)
     mzz = mlz + pos["gz"] * hz
-    mxx = iota((mx, my, mz), 0) - hx + pos["gx"] * hx
     middle_in = (
         (mr >= 0) & (mr < hy * sizes["gy"]) & (mzz >= 0) & (mzz < hz * sizes["gz"])
-        & (mxx >= 0) & (mxx < hx * sizes["gx"]) & (mlz >= -H) & (mlz < hz + H)
+        & (mlz >= -H) & (mlz < hz + H)
     )
+
+    def middle_plane_in(i):
+        x = i - hx + pos["gx"] * hx
+        return (x >= 0) & (x < hx * sizes["gx"])
 
     jj = iota((mz, mz), 1)
     back_z = interpolate_weight(jj + pz * hz, iota((mz, mz), 0))
@@ -339,46 +341,56 @@
                     p = (i - H) % cx
                     ks[f, i, :, cz_:ez] = shift(merged, 1, H + 2 * H * (f * cx + p))
 
-    def weights(i, carry):
-        k = ks[0, i]
-        after = 0.5 * (k + ks[0, i + 1])
+    fine_w = (wx, wy, wz, dg, iv)
+    middle_w = (mwx, mwy, mwz, mdg, miv)
+
+    def set_weights(w, k_of, i, inside):
+        ax, ay, az, diag_ref, inverse_ref = w
+        k = k_of(i)
+        after = 0.5 * (k + k_of(i + 1))
         a = 0.5 * (k + shift(k, 0, 1))
         b = 0.5 * (k + shift(k, 1, 1))
-        diag = (wx[i - 1] + after) + (a + shift(a, 0, -1)) + (b + shift(b, 1, -1))
-        wx[i] = after
-        wy[i] = a
-        wz[i] = b
-        inverse = jnp.where(fine_in & plane_in(i), 1.0 / diag, 0.0)
-        iv[i] = inverse
-        ua[i] = omega_first * ks[1, i] * inverse
-        return carry
-
-    def around(u, i):
+        diag = (ax[i - 1] + after) + (a + shift(a, 0, -1)) + (b + shift(b, 1, -1))
+        ax[i] = after
+        ay[i] = a
+        az[i] = b
+        diag_ref[i] = diag
+        inverse = jnp.where(inside, 1.0 / diag, 0.0)
+        inverse_ref[i] = inverse
+        return inverse
+
+    def around(w, u, i):
         v = u[i]
-        a, b = wy[i], wz[i]
-        total = wx[i] * u[i + 1] + wx[i - 1] * u[i - 1]
+        a, b = w[1][i], w[2][i]
+        total = w[0][i] * u[i + 1] + w[0][i - 1] * u[i - 1]
         total = total + (a * shift(v, 0, 1) + shift(a * v, 0, -1))
         total = total + (b * shift(v, 1, 1) + shift(b * v, 1, -1))
         return v, total
 
-    def fine_sweep(u, i, omega):
-        v, total = around(u, i)
-        return (1.0 - omega) * v + omega * (ks[1, i] + total) * iv[i]
-
-    def pre(i, carry):
-        ub[i] = fine_sweep(ua, i, omega_second)
-        return carry
-
-
-    def leftover(i, carry):
-        v, total = around(ub, i)
-        inverse = iv[i]
-        diag = wx[i] + wx[i - 1] + (wy[i] + shift(wy[i], 0, -1)) + (wz[i] + shift(wz[i], 1, -1))
-        left[i] = jnp.where(inverse > 0.0, ks[1, i] - diag * v + total, 0.0)
-        return carry
+    def plane_sweep(w, f, u, i, omega):
+        v, total = around(w, u, i)
+        return (1.0 - omega) * v + omega * (f + total) * w[4][i]
+
+    def plane_left(w, f, u, i):
+        v, total = around(w, u, i)
+        return jnp.where(w[4][i] > 0.0, f - w[3][i] * v + total, 0.0)
 
     def run(low, high, body):
-        lax.fori_loop(low, high, body, 0, unroll=2)
+        def step(i, carry):
+            body(i)
+            return carry
+
+        lax.fori_loop(low, high, step, 0, unroll=2)
+
+    def weights(i):
+        inverse = set_weights(fine_w, lambda j: ks[0, j], i, fine_in & plane_in(i))
+        ua[i] = omega_first * ks[1, i] * inverse
+
+    def pre(i):
+        ub[i] = plane_sweep(fine_w, ks[1, i], ua, i, omega_second)
+
+    def leftover(i):
+        left[i] = plane_left(fine_w, ks[1, i], ub, i)
 
     last_own = H + cx - 1
     finish_recv(fine_round, lambda offset: offset[0] == 0)
@@ -437,10 +449,16 @@
     def sweep(w, inverse, v, f, omega):
         return (1.0 - omega) * v + omega * (f + neighbours(w, v)) * inverse
 
-    mk = middle_finish(0, coeff_round)
-    mw = faces(mk)
-    mdiag = diagonal(mw)
-    miv = jnp.where(middle_in, 1.0 / mdiag, 0.0)
+    def put_coeff(i, values):
+        mk[i] = values
+
+    middle_finish(0, coeff_round, put_coeff)
+    mwx[0] = 0.5 * (mk[0] + mk[1])
+
+    def middle_weights(i):
+        set_weights(middle_w, lambda j: mk[j], i, middle_in & middle_plane_in(i))
+
+    run(1, mx - 1, middle_weights)
 
     for copy in gather_coeff:
         copy.wait_recv()
@@ -464,15 +482,27 @@
     finish_send(coeff_round)
     for copy in gather_coeff:
         copy.wait_send()
-    mf = middle_finish(1, rhs_round)
-    m1 = omega_first * mf * miv
-    m2 = sweep(mw, miv, m1, mf, omega_second)
-    mleft = jnp.where(middle_in, mf - mdiag * m2 + neighbours(mw, m2), 0.0)
+
+    def put_rhs(i, values):
+        mf[i] = values
+        if 1 <= i < mx - 1:
+            va[i] = omega_first * values * miv[i]
+
+    middle_finish(1, rhs_round, put_rhs)
+
+    def middle_pre(i):
+        vb[i] = plane_sweep(middle_w, mf[i], va, i, omega_second)
+
+    def middle_leftover(i):
+        va[i] = plane_left(middle_w, mf[i], vb, i)
+
+    run(2, mx - 2, middle_pre)
+    run(3, mx - 3, middle_leftover)
 
     pieces = []
     for i in range(qx):
         c = hx + 2 * i
-        cs[i] = (mleft[c - 1] + mleft[c + 2]) * 0.5 + (mleft[c] + mleft[c + 1]) * 1.5
+        cs[i] = (va[c - 1] + va[c + 2]) * 0.5 + (va[c] + va[c + 1]) * 1.5
         pieces.append(restrict_rows(lambda first: cs[i, pl.ds(first, qy, stride=2), :]))
     rhs = times(jnp.concatenate(pieces, axis=0), to_coarse_z)
     for i in range(qx):
@@ -488,17 +518,28 @@
     flat = c2.reshape(nx * ny, mz)
     correction = weigh(back_xy, times(flat, back_z))
     for i in range(hx):
-        fixed = m2[hx + i, T : T + hy, :] + correction[i * hy : (i + 1) * hy]
+        fixed = vb[hx + i, T : T + hy, :] + correction[i * hy : (i + 1) * hy]
         mid[2, hx + i, T : T + hy, :] = fixed
     last_round = middle_start(2)
     for copy in gather_rhs:
         copy.wait_send()
-    m3 = middle_finish(2, last_round)
-    m4 = sweep(mw, miv, m3, mf, omega_first)
-    m5 = sweep(mw, miv, m4, mf, omega_second)
+
+    def put_last(i, values):
+        vc[i] = values
+
+    middle_finish(2, last_round, put_last)
+
+    def middle_post_first(i):
+        va[i] = plane_sweep(middle_w, mf[i], vc, i, omega_first)
+
+    def middle_post_second(i):
+        vb[i] = plane_sweep(middle_w, mf[i], va, i, omega_second)
+
+    run(1, mx - 1, middle_post_first)
+    run(2, mx - 2, middle_post_second)
 
     low = hx - 2
-    spread = times(m5[low : 2 * hx + 2].reshape((hx + 4) * my, mz), to_fine_z)
+    spread = times(vb[low : 2 * hx + 2].reshape((hx + 4) * my, mz), to_fine_z)
     for i in range(2, ex - 2):
         c = (i - H + 64) // 2 - 32 + hx - low
         other = c - 1 if i % 2 == 0 else c + 1
@@ -515,17 +556,15 @@
         fresh = jnp.concatenate([fs[0, i - 2, rows, :], fs[1, i - 2, rows, :]], axis=1)
         ua[i] = jnp.where(fine_in & plane_in(i), ub[i] + fresh, 0.0)
 
-    def post(i, carry):
-        ub[i] = fine_sweep(ua, i, omega_first)
-        return carry
-
-    lax.fori_loop(3, ex - 3, post, 0, unroll=2)
-
-    def last(i, carry):
-        out_ref[i - H] = fine_sweep(ub, i, omega_second)[T : T + cy, 0:cz_]
-        return carry
-
-    lax.fori_loop(H, H + cx, last, 0, unroll=2)
+    def post(i):
+        ub[i] = plane_sweep(fine_w, ks[1, i], ua, i, omega_first)
+
+    def last(i):
+        result = plane_sweep(fine_w, ks[1, i], ub, i, omega_second)
+        out_ref[i - H] = result[T : T + cy, 0:cz_]
+
+    run(3, ex - 3, post)
+    run(H, H + cx, last)
     finish_send(last_round)
 
 
@@ -548,16 +587,11 @@
                 vmem((cy, cz), F32),
                 vmem((3, cy + 2 * T, cz), F32),
                 vmem((3, cy + 2 * T, cz), F32),
-                vmem(fine, F32),
-                vmem(fine, F32),
-                vmem(fine, F32),
-                vmem(fine, F32),
-                vmem(fine, F32),
-                vmem(fine, F32),
-                vmem(fine, F32),
+                *[vmem(fine, F32)] * 8,
                 vmem((2, cx // 2, cy + 2 * T, cz), F32),
                 vmem((2, cx + 4, 2 * mid[1], cz), F32),
                 vmem((cx // 4, mid[1], cz), F32),
+                *[vmem(mid, F32)] * 10,
                 vmem((3,) + mid, F32),
                 vmem((3, cy // 2, cz), F32),
                 vmem((3, 3) + mid[1:], F32),

time: 30.3 us -> 31.3 us (1.033)
  Pallas kernels: 29.5 us -> 30.5 us
    pallas_call x1, Pallas kernels: 29.5 us -> 30.5 us  [local(): call(*(pltpu.with_memory_space_constraint(v, pltpu.HBM) for v in (source,...]
where the time goes in v5:
time: 31.3 us; the launch traced here: 31.1 us
  Pallas kernels  30.5 us (97%)
  local copies, waits for them, and re-layouts  0.66 us (2%)
    pallas_call x1, Pallas kernels, local(): call(*(pltpu.with_memory_space_constraint(v, pltpu.HBM) for v in (source,...  30.5 us
    unnamed x1, local copies, waits for them, and re-layouts  0.66 us

profile of v5, /device:TPU:1, one launch (start us, length us, event | category | flops | bytes accessed | tf_op | source)
XLA Modules:
  0.0 31.1 jit_solution(4269851948899742333)
XLA Ops:
  0.0 30.5 %shard_map.28 = f32[8,32,128]{2,1,0:T(8,128)S(1)} custom-call(f32[8,32,128]{2,1,0:T(8,128)} %s_ref.1, f32[8,32,128]{2,1,0:T(8,128)} %k_ref.1), custom_call_target="tpu_custom_call" | custom-call | tf_op jit(solution)/shard_map/pallas_call | solution.py:608
  30.5 0.7 %copy.4 = f32[8,32,128]{2,1,0:T(8,128)} copy(f32[8,32,128]{2,1,0:T(8,128)S(1)} %shard_map.28) | data formatting | bytes 262144

commit v6 on v5

--- a/solution.py
+++ b/solution.py
@@ -376,11 +376,8 @@
         return jnp.where(w[4][i] > 0.0, f - w[3][i] * v + total, 0.0)
 
     def run(low, high, body):
-        def step(i, carry):
+        for i in range(low, high):
             body(i)
-            return carry
-
-        lax.fori_loop(low, high, step, 0, unroll=2)
 
     def weights(i):
         inverse = set_weights(fine_w, lambda j: ks[0, j], i, fine_in & plane_in(i))

time: 31.3 us -> 28.9 us (0.923)
  Pallas kernels: 30.5 us -> 28.1 us
    pallas_call x1, Pallas kernels: 30.5 us -> 28.1 us  [local(): call(*(pltpu.with_memory_space_constraint(v, pltpu.HBM) for v in (source,...]
where the time goes in v6:
time: 28.9 us; the launch traced here: 28.8 us
  Pallas kernels  28.1 us (97%)
  local copies, waits for them, and re-layouts  0.66 us (2%)
    pallas_call x1, Pallas kernels, local(): call(*(pltpu.with_memory_space_constraint(v, pltpu.HBM) for v in (source,...  28.1 us
    unnamed x1, local copies, waits for them, and re-layouts  0.66 us

profile of v6, /device:TPU:1, one launch (start us, length us, event | category | flops | bytes accessed | tf_op | source)
XLA Modules:
  0.0 28.8 jit_solution(558117689994253850)
XLA Ops:
  0.0 28.1 %shard_map.28 = f32[8,32,128]{2,1,0:T(8,128)S(1)} custom-call(f32[8,32,128]{2,1,0:T(8,128)} %s_ref.1, f32[8,32,128]{2,1,0:T(8,128)} %k_ref.1), custom_call_target="tpu_custom_call" | custom-call | tf_op jit(solution)/shard_map/pallas_call | solution.py:605
  28.1 0.7 %copy.4 = f32[8,32,128]{2,1,0:T(8,128)} copy(f32[8,32,128]{2,1,0:T(8,128)S(1)} %shard_map.28) | data formatting | bytes 262144

commit v7 on v6

--- a/solution.py
+++ b/solution.py
@@ -520,6 +520,7 @@
     last_round = middle_start(2)
     for copy in gather_rhs:
         copy.wait_send()
+    finish_send(last_round)
 
     def put_last(i, values):
         vc[i] = values
@@ -562,7 +563,6 @@
 
     run(3, ex - 3, post)
     run(H, H + cx, last)
-    finish_send(last_round)
 
 
 def solution(mesh):

time: 28.9 us -> 28.9 us (level)
  no operation moved by 1% of the time
where the time goes in v7:
time: 28.9 us; the launch traced here: 28.8 us
  Pallas kernels  28.1 us (97%)
  local copies, waits for them, and re-layouts  0.66 us (2%)
    pallas_call x1, Pallas kernels, local(): call(*(pltpu.with_memory_space_constraint(v, pltpu.HBM) for v in (source,...  28.1 us
    unnamed x1, local copies, waits for them, and re-layouts  0.66 us

profile of v7, /device:TPU:1, one launch (start us, length us, event | category | flops | bytes accessed | tf_op | source)
XLA Modules:
  0.0 28.8 jit_solution(17345141730551327302)
XLA Ops:
  0.0 28.1 %shard_map.28 = f32[8,32,128]{2,1,0:T(8,128)S(1)} custom-call(f32[8,32,128]{2,1,0:T(8,128)} %s_ref.1, f32[8,32,128]{2,1,0:T(8,128)} %k_ref.1), custom_call_target="tpu_custom_call" | custom-call | tf_op jit(solution)/shard_map/pallas_call | solution.py:605
  28.1 0.7 %copy.4 = f32[8,32,128]{2,1,0:T(8,128)} copy(f32[8,32,128]{2,1,0:T(8,128)S(1)} %shard_map.28) | data formatting | bytes 262144
